TPU v7x, 32 devices: a whole 2x2x4 slice. The times are simulated.
32 devices in a mesh: seq: 16 (over z, x, core), head: 2 (over y).
Axes of the slice: x: 2, y: 2, z: 4, core: 2. Of those that a mesh axis runs over, the one named last changes fastest.
Arguments:
- projected: float32 [4096, 2560], P(('seq', 'head')), may hold values from -6 to 6
- out_grads: float32 [4096, 2048], P(('seq', 'head')), may hold values from -6 to 6
- conv_weight: float32 [3, 2560], replicated, may hold values from -2.4 to 2.4
- doc_lengths: int32 [4], replicated, may hold values from 1 to 2048, 4096 in all
Outputs:
- grad_projected: float32 [4096, 2560], P(('seq', 'head'))
- grad_conv: float32 [3, 2560], replicated
Inputs may be any that keep to these rules, and one draw needn't show every extreme that they name: `doc_lengths`: the 4 documents fill the 4096 tokens end to end; the longest holds exactly half of 4096 tokens.
All inputs are finite; a program needn't handle non-finite values.
Results may differ from a plain program's by a relative error of at most 0.0003.
Values sent between devices are 32-bit elements; how exact they have to be, the bound alone decides.
A program may use at most 128 MiB of HBM per device.

v0:
```python
import math

import jax
import jax.numpy as jnp
import numpy as np
from jax import lax
from jax.sharding import PartitionSpec as P

KEY_DIM = 16
HEAD_DIM = 128


HIGHEST = lax.Precision.HIGHEST


def carried_in(x, axis, combine, identity, reverse):
    length, here = (lax.axis_size(axis), lax.axis_index(axis))
    everything = jax.tree.map(lambda part: lax.all_gather(part, axis), x)
    start = jax.tree.map(
        lambda part, zero: jnp.broadcast_to(jnp.asarray(zero, part.dtype), part.shape), x, identity
    )

    def lap(k, before):
        at = length - 1 - k if reverse else k
        reached = at > here if reverse else at < here
        new = combine(before, jax.tree.map(lambda part: part[at], everything))
        return jax.tree.map(lambda a, b: jnp.where(reached, a, b), new, before)

    return lax.fori_loop(0, length, lap, start)


def passed_along(value, axis, steps):
    count = lax.axis_size(axis)
    initial, last = (max(0, -steps), min(count, count - steps))
    return lax.ppermute(value, axis, [(source, source + steps) for source in range(initial, last)])


def feature_map(columns):
    key_size = columns.shape[1]
    upper_i, upper_j = np.triu_indices(key_size)
    factors = np.where(upper_i == upper_j, 1.0 / math.sqrt(2.0), 1.0).astype(np.float32)
    products = columns[:, upper_i, :] * columns[:, upper_j, :] * jnp.asarray(factors)[None, :, None]
    constant = jnp.ones((columns.shape[0], 1, columns.shape[2]), jnp.float32)
    return jnp.concatenate([constant, columns, products], axis=1)


def doc_place(doc_lengths, anchor, amount):
    positions = anchor + jnp.arange(amount, dtype=jnp.int32)
    starts = jnp.cumsum(doc_lengths) - doc_lengths
    begins = jnp.max(jnp.where(starts[None, :] <= positions[:, None], starts[None, :], 0), axis=1)
    return (begins, positions - begins)


def conv_forward(signal, leading, weights, offsets):
    row_count = signal.shape[0]
    behind = jnp.concatenate([leading, signal], axis=0)
    back_one = behind[1 : row_count + 1] * (offsets[0:row_count] >= 1).astype(jnp.float32)[:, None]
    back_two = behind[0:row_count] * (offsets[0:row_count] >= 2).astype(jnp.float32)[:, None]
    return weights[0] * signal + weights[1] * back_one + weights[2] * back_two


def conv_backward(grad_rows, trailing, signal, leading, weights, offsets):
    row_count = grad_rows.shape[0]
    ahead_rows = jnp.concatenate([grad_rows, trailing], axis=0)
    ahead_one = (
        ahead_rows[1 : row_count + 1]
        * (offsets[1 : row_count + 1] >= 1).astype(jnp.float32)[:, None]
    )
    ahead_two = (
        ahead_rows[2 : row_count + 2]
        * (offsets[2 : row_count + 2] >= 2).astype(jnp.float32)[:, None]
    )
    grad_signal = weights[0] * grad_rows + weights[1] * ahead_one + weights[2] * ahead_two
    behind = jnp.concatenate([leading, signal], axis=0)
    own_one = (offsets[0:row_count] >= 1).astype(jnp.float32)[:, None]
    own_two = (offsets[0:row_count] >= 2).astype(jnp.float32)[:, None]
    grad_weights = jnp.stack(
        [
            jnp.sum(grad_rows * signal, axis=0),
            jnp.sum(grad_rows * behind[1 : row_count + 1] * own_one, axis=0),
            jnp.sum(grad_rows * behind[0:row_count] * own_two, axis=0),
        ],
        axis=0,
    )
    return (grad_signal, grad_weights)


def combine(earlier, following):
    carry_keep = 1.0 - following[2]
    return (
        following[0] + carry_keep[:, None, None] * earlier[0],
        following[1] + carry_keep[:, None] * earlier[1],
        jnp.maximum(earlier[2], following[2]),
    )


def attention_grads(mixed_rows, out_flat, begins, stretch_start):
    length = mixed_rows.shape[0]
    head_width = 2 * KEY_DIM + HEAD_DIM
    local_heads = mixed_rows.shape[1] // head_width
    block_len = min(128, length)
    blocks = length // block_len
    scale_key = KEY_DIM ** (-0.25)
    shaped = mixed_rows.reshape(length, local_heads, head_width)
    query_cols = jnp.transpose(shaped[:, :, :KEY_DIM], (1, 2, 0)) * scale_key
    key_cols = jnp.transpose(shaped[:, :, KEY_DIM : 2 * KEY_DIM], (1, 2, 0)) * scale_key
    values = shaped[:, :, 2 * KEY_DIM :]
    upstream = out_flat.reshape(length, local_heads, HEAD_DIM)
    query_feat, query_pull = jax.vjp(feature_map, query_cols)
    key_feat, key_pull = jax.vjp(feature_map, key_cols)
    feat_count = query_feat.shape[1]
    last_begin = begins[length - 1]
    has_start = (last_begin >= stretch_start).astype(jnp.float32).reshape(1)
    tail_mask = (begins == last_begin).astype(jnp.float32)
    tail_feat = key_feat * tail_mask[None, None, :]
    tail_state = jnp.einsum("hfl,lhe->hfe", tail_feat, values, precision=HIGHEST)
    tail_norm = jnp.sum(tail_feat, axis=2)
    identity = (jnp.zeros_like(tail_state), jnp.zeros_like(tail_norm), jnp.zeros((1,), jnp.float32))
    prefix = carried_in((tail_state, tail_norm, has_start), "seq", combine, identity, False)
    causal = jnp.arange(block_len)[:, None] >= jnp.arange(block_len)[None, :]
    indices = jnp.arange(blocks, dtype=jnp.int32)

    def forward_block(carried, block_index):
        carry_state, carry_norm = carried
        offset_rows = block_index * block_len
        block_start = stretch_start + offset_rows
        query_blk = lax.dynamic_slice_in_dim(query_feat, offset_rows, block_len, 2)
        key_blk = lax.dynamic_slice_in_dim(key_feat, offset_rows, block_len, 2)
        value_blk = lax.dynamic_slice_in_dim(values, offset_rows, block_len, 0)
        doc_blk = lax.dynamic_slice_in_dim(begins, offset_rows, block_len, 0)
        allowed = causal & (doc_blk[:, None] == doc_blk[None, :])
        scores = jnp.where(
            allowed[None], jnp.einsum("hft,hfs->hts", query_blk, key_blk, precision=HIGHEST), 0.0
        )
        from_carry = (doc_blk < block_start).astype(jnp.float32)
        numerator = jnp.einsum("hts,she->the", scores, value_blk, precision=HIGHEST) + from_carry[
            :, None, None
        ] * jnp.einsum("hft,hfe->the", query_blk, carry_state, precision=HIGHEST)
        denominator = jnp.sum(scores, axis=2) + from_carry[None, :] * jnp.einsum(
            "hft,hf->ht", query_blk, carry_norm, precision=HIGHEST
        )
        block_tail = (doc_blk == doc_blk[block_len - 1]).astype(jnp.float32)
        carry_keep = (doc_blk[block_len - 1] < block_start).astype(jnp.float32)
        tail_keys = key_blk * block_tail[None, None, :]
        next_state = (
            jnp.einsum("hfs,she->hfe", tail_keys, value_blk, precision=HIGHEST)
            + carry_keep * carry_state
        )
        next_norm = jnp.sum(tail_keys, axis=2) + carry_keep * carry_norm
        return ((next_state, next_norm), (numerator, denominator, carry_state, carry_norm, scores))

    forward_out = lax.scan(forward_block, (prefix[0], prefix[1]), indices)
    numerators, denominators, states, norms, kept_scores = forward_out[1]
    denom_rows = jnp.transpose(denominators, (0, 2, 1)).reshape(length, local_heads)
    attended = numerators.reshape(length, local_heads, HEAD_DIM) / denom_rows[:, :, None]
    grad_num = upstream / denom_rows[:, :, None]
    scalar_grad = -jnp.sum(upstream * attended, axis=2) / denom_rows
    lead_mask = (begins < stretch_start).astype(jnp.float32)
    lead_feat = query_feat * lead_mask[None, None, :]
    lead_state = jnp.einsum("hfl,lhe->hfe", lead_feat, grad_num, precision=HIGHEST)
    lead_norm = jnp.einsum("hfl,lh->hf", lead_feat, scalar_grad, precision=HIGHEST)
    suffix = carried_in((lead_state, lead_norm, has_start), "seq", combine, identity, True)

    def backward_block(carried, inputs):
        back_state, back_norm = carried
        block_index, carry_state, carry_norm, scores = inputs
        offset_rows = block_index * block_len
        block_start = stretch_start + offset_rows
        query_blk = lax.dynamic_slice_in_dim(query_feat, offset_rows, block_len, 2)
        key_blk = lax.dynamic_slice_in_dim(key_feat, offset_rows, block_len, 2)
        value_blk = lax.dynamic_slice_in_dim(values, offset_rows, block_len, 0)
        doc_blk = lax.dynamic_slice_in_dim(begins, offset_rows, block_len, 0)
        grad_blk = lax.dynamic_slice_in_dim(grad_num, offset_rows, block_len, 0)
        scalar_blk = lax.dynamic_slice_in_dim(scalar_grad, offset_rows, block_len, 0)
        scalar_cols = scalar_blk.T
        allowed = causal & (doc_blk[:, None] == doc_blk[None, :])
        dscores = jnp.where(
            allowed[None],
            jnp.einsum("the,she->hts", grad_blk, value_blk, precision=HIGHEST)
            + scalar_cols[:, :, None],
            0.0,
        )
        from_carry = (doc_blk < block_start).astype(jnp.float32)
        block_tail = (doc_blk == doc_blk[block_len - 1]).astype(jnp.float32)
        carry_keep = (doc_blk[block_len - 1] < block_start).astype(jnp.float32)
        grad_query = jnp.einsum("hts,hfs->hft", dscores, key_blk, precision=HIGHEST) + from_carry[
            None, None, :
        ] * (
            jnp.einsum("hfe,the->hft", carry_state, grad_blk, precision=HIGHEST)
            + carry_norm[:, :, None] * scalar_cols[:, None, :]
        )
        grad_key = jnp.einsum("hts,hft->hfs", dscores, query_blk, precision=HIGHEST) + block_tail[
            None, None, :
        ] * (
            jnp.einsum("hfe,she->hfs", back_state, value_blk, precision=HIGHEST)
            + back_norm[:, :, None]
        )
        grad_value = jnp.einsum("hts,the->she", scores, grad_blk, precision=HIGHEST) + block_tail[
            :, None, None
        ] * jnp.einsum("hfs,hfe->she", key_blk, back_state, precision=HIGHEST)
        lead_blk = query_blk * from_carry[None, None, :]
        next_state = (
            jnp.einsum("hft,the->hfe", lead_blk, grad_blk, precision=HIGHEST)
            + carry_keep * back_state
        )
        next_norm = (
            jnp.einsum("hft,th->hf", lead_blk, scalar_blk, precision=HIGHEST)
            + carry_keep * back_norm
        )
        return ((next_state, next_norm), (grad_query, grad_key, grad_value))

    swept_back = lax.scan(
        backward_block, (suffix[0], suffix[1]), (indices, states, norms, kept_scores), reverse=True
    )
    grad_qblocks, grad_kblocks, grad_vblocks = swept_back[1]
    query_grad = jnp.transpose(grad_qblocks, (1, 2, 0, 3)).reshape(local_heads, feat_count, length)
    key_grad = jnp.transpose(grad_kblocks, (1, 2, 0, 3)).reshape(local_heads, feat_count, length)
    value_grad = grad_vblocks.reshape(length, local_heads, HEAD_DIM)
    query_in = jnp.transpose(query_pull(query_grad)[0] * scale_key, (2, 0, 1))
    key_in = jnp.transpose(key_pull(key_grad)[0] * scale_key, (2, 0, 1))
    return jnp.concatenate([query_in, key_in, value_grad], axis=2).reshape(
        length, local_heads * head_width
    )


def on_device(projected, out_grads, conv_weight, doc_lengths):
    row_count = projected.shape[0]
    head_count = lax.axis_size("head")
    seq_index = lax.axis_index("seq")
    head_index = lax.axis_index("head")
    group_len = row_count * head_count
    token_base = (seq_index * head_count + head_index) * row_count
    stretch_start = seq_index * group_len
    token_begins, token_offsets = doc_place(doc_lengths, token_base, row_count + 2)
    leading = passed_along(projected[row_count - 2 :], ("seq", "head"), 1)
    outgoing = conv_forward(projected, leading, conv_weight, token_offsets)
    arrived, upstream = (
        lax.all_to_all(outgoing, "head", split_axis=1, concat_axis=0, tiled=True),
        lax.all_to_all(out_grads, "head", split_axis=1, concat_axis=0, tiled=True),
    )
    group_begins, group_offsets = doc_place(doc_lengths, stretch_start, group_len + 2)
    grad_mixed = attention_grads(arrived, upstream, group_begins[:group_len], stretch_start)
    returned = lax.all_to_all(grad_mixed, "head", split_axis=0, concat_axis=1, tiled=True)
    trailing = passed_along(returned[:2], ("seq", "head"), -1)
    grad_projected, weight_part = conv_backward(
        returned, trailing, projected, leading, conv_weight, token_offsets
    )
    grad_conv = lax.psum(weight_part, ("seq", "head"))
    return (grad_projected, grad_conv)


def solution(mesh):
    return jax.shard_map(
        on_device,
        mesh=mesh,
        in_specs=(P(("seq", "head"), None), P(("seq", "head"), None), P(), P()),
        out_specs=(P(("seq", "head"), None), P()),
        check_vma=False,
    )
```

profile of v0, /device:TPU:0, one launch (start us, length us, event | category | flops | bytes accessed | tf_op | source)
XLA Modules:
  0.0 652.8 jit_solution(1036977616029527161)
XLA Ops:
  8.1 4.9 collective-permute-start
  18.5 3.1 multiply_add_fusion.1
  21.6 3.8 all-to-all-start
  26.9 15.1 %all-to-all-done = f32[128,2,1280]{0,2,1:T(8,128)S(1)} async-done(((f32[128,2,1280]{0,2,1:T(8,128)}), f32[128,2,1280]{0,2,1:T(8,128)S(1)}, u32[]{:S(2)}, u32[]{:S(2)}) %all-to-all-start) | async-done | bytes 1310752 | tf_op jit(solution)/shard_map/all_to_all | solution.py:238
  42.0 4.7 copy.232
  54.2 2.2 fusion.90
  56.4 2.3 pad_maximum_fusion.3
  62.6 3.7 all-to-all-start.1
  68.6 32.7 %all-reduce = f32[16]{0:T(128)S(1)} all-reduce(f32[16]{0:T(128)S(1)} %dynamic-update-slice), channel_id=1, replica_groups=mesh['seq'=16,'head'=2] {'seq'}, use_global_device_ids=true, to_apply=%add | all-reduce | flops 16 | bytes 128
  105.9 2.6 copy.287
  108.6 18.5 %all-gather.1 = f32[128,153]{1,0:T(8,128)S(1)} all-gather(f32[8,153]{1,0:T(8,128)S(1)} %copy.239), channel_id=3, replica_groups=mesh['seq'=16,'head'=2] {'seq'}, dimensions={0}, use_global_device_ids=true | all-gather | bytes 83232 | tf_op jit(solution)/shard_map/all_gather | solution.py:18
  127.0 24.2 %all-gather.7.cloned.1.call-done = f32[128,153,128]{2,0,1:T(8,128)} async-done(((f32[8,153,128]{2,0,1:T(8,128)}), f32[128,153,128]{2,0,1:T(8,128)}) %all-gather.7.cloned.1.call-update) | async-done | bytes 10027024 | tf_op jit(solution)/shard_map/all_gather | solution.py:18
  151.2 83.8 %while.82 = (s32[]{:T(128)}, f32[8,153,128]{2,1,0:T(8,128)S(1)}, f32[8,153]{1,0:T(8,128)S(1)}, s32[]{:T(128)}, f32[16,8,153,128]{3,1,0,2:T(8,128)}, /*index=5*/f...) while((s32[]{:T(128)}, f32[8,153,128]{2,1,0:T(8,128)S(1)}, ...), condition=%wide.region_5.6_spmd.clone, body=%wide.region_4.5_spmd.clone.sunk | while | flops 631589 | bytes 3148271 | solution.py:29
  159.0 2.1 fusion.199
  174.7 2.1 fusion.199
  179.9 2.1 fusion.199
  190.4 2.1 fusion.199
  195.6 2.1 fusion.199
  237.3 34.5 %while.80 = (s32[]{:T(128)}, f32[8,153,128]{2,1,0:T(8,128)S(1)}, f32[8,153]{1,0:T(8,128)S(1)}, f32[2,128,8,128]{3,2,1,0:T(8,128)}, f32[2,8,128]{2,1,0:T(8,128)S(...) while((s32[]{:T(128)}, f32[8,153,128]{2,1,0:T(8,128)S(1)}, ...), condition=%wide.region_9.10_spmd.clone, body=%wide.region_6.9_spmd.clone.sunk | while | flops 926510784 | bytes 26628632 | solution.py:152
  241.7 2.7 fusion.169
  259.0 2.7 fusion.169
  272.0 3.0 bitcast_divide_fusion
  278.0 2.6 copy.245
  281.1 2.8 fusion.85
  283.9 20.0 %all-gather.3 = f32[128,153]{1,0:T(8,128)S(1)} all-gather(f32[8,153]{1,0:T(8,128)S(1)} %bitcast.287), channel_id=5, replica_groups=mesh['seq'=16,'head'=2] {'seq'}, dimensions={0}, use_global_device_ids=true | all-gather | bytes 83232 | tf_op jit(solution)/shard_map/all_gather | solution.py:18
  303.9 61.4 %all-gather.9.cloned.1.call-done = f32[128,153,128]{2,0,1:T(8,128)} async-done(((f32[8,153,128]{2,0,1:T(8,128)}), f32[128,153,128]{2,0,1:T(8,128)}) %all-gather.9.cloned.1.call-update) | async-done | bytes 10027024 | tf_op jit(solution)/shard_map/all_gather | solution.py:18
  365.2 105.3 %while.83 = (s32[]{:T(128)}, f32[8,153,128]{2,1,0:T(8,128)S(1)}, f32[8,153]{1,0:T(8,128)S(1)}, s32[]{:T(128)}, f32[16,8,153,128]{3,1,0,2:T(8,128)}, /*index=5*/f...) while((s32[]{:T(128)}, f32[8,153,128]{2,1,0:T(8,128)S(1)}, ...), condition=%wide.region_12.13_spmd.clone, body=%wide.region_11.12_spmd.clone.sunk | while | flops 631593 | bytes 3148333 | solution.py:29
  376.8 2.1 fusion.202
  382.9 2.1 fusion.202
  389.0 2.1 fusion.202
  395.0 2.1 fusion.202
  401.1 2.1 fusion.202
  407.1 2.1 fusion.202
  413.2 2.1 fusion.202
  419.2 2.1 fusion.202
  425.3 2.1 fusion.202
  431.4 2.1 fusion.202
  437.4 2.1 fusion.202
  443.5 2.1 fusion.202
  449.5 2.1 fusion.202
  455.6 2.1 fusion.202
  461.6 2.1 fusion.202
  467.7 2.1 fusion.202
  474.0 47.7 %while.81 = (s32[]{:T(128)}, f32[8,153,128]{2,1,0:T(8,128)S(1)}, f32[8,153]{1,0:T(8,128)S(1)}, f32[2,8,153,128]{3,2,1,0:T(8,128)}, f32[2,8,153,128]{3,2,1,0:T(8,...) while((s32[]{:T(128)}, f32[8,153,128]{2,1,0:T(8,128)S(1)}, ...), condition=%wide.region_14.15_spmd.clone, body=%wide.region_13.14_spmd.clone.sunk | while | flops 1850722176 | bytes 32832120 | solution.py:212
  476.6 2.2 convolution_bitcast_fusion.5
  478.8 2.7 fusion.197
  485.6 2.4 fusion.192
  489.2 2.1 fusion.194
  500.4 2.2 convolution_bitcast_fusion.5
  502.7 2.7 fusion.197
  509.5 2.4 fusion.192
  513.1 2.1 fusion.194
  515.9 2.1 fusion.196
  521.7 2.2 copy.327
  524.0 2.2 copy.328
  528.1 12.0 %scatter_fusion = f32[8,16,256]{2,0,1:T(8,128)S(1)} fusion(f32[8,16,256]{2,0,1:T(8,128)S(1)} %split.16, s32[136]{0:T(256)S(1)} %copy-done.32, f32[136,8,256]{2,1,0:T(8,128)} %get-tuple-element.1251), kind=kCustom, calls=%fused_computation.4 | custom fusion | flops 278528 | bytes 3342880 | tf_op jit(solution)/shard_map/transpose(jvp())/scatter-add | solution.py:42
  540.1 12.0 %scatter_fusion.1 = f32[8,16,256]{2,0,1:T(8,128)S(1)} fusion(f32[8,16,256]{2,0,1:T(8,128)S(1)} %broadcast.118.clone.1, s32[136]{0:T(256)S(1)} %copy-done.34, f32[136,8,256]{2,1,0:T(8,128)} %get-tuple-element.1250), kind=kCustom, calls=%fused_computation.5 | custom fusion | flops 278528 | bytes 3342880 | tf_op jit(solution)/shard_map/transpose(jvp())/scatter-add | solution.py:42
  553.5 6.1 scatter_fusion.3
  559.7 5.9 scatter_fusion.2
  567.0 2.7 pad_maximum_fusion
  572.2 21.0 %all_to_all.51 = f32[2,128,1280]{1,2,0:T(8,128)S(1)} all-to-all(f32[2,128,1280]{1,2,0:T(8,128)} %copy.260), channel_id=1, replica_groups=mesh['seq'=16,'head'=2] {'head'}, dimensions={0} | all-to-all | bytes 2621440 | tf_op jit(solution)/shard_map/all_to_all | solution.py:243
  593.2 2.2 multiply_reduce_fusion.2
  597.2 41.2 %psum.7 = f32[3,2560]{1,0:T(4,128)} all-reduce(f32[3,2560]{1,0:T(4,128)S(1)} %pad_maximum_fusion.5), channel_id=1, replica_groups=mesh['seq'=16,'head'=2] {'seq','head'}, use_global_device_ids=true, to_apply=%region_22.23 | all-reduce | flops 7680 | bytes 61440 | tf_op jit(solution)/shard_map/psum | solution.py:248
  639.9 4.4 fusion.79
  (361 shorter events, 232.6 us)
Async XLA Ops:
  8.1 9.9 %collective-permute-start = (f32[2,2560]{1,0:T(2,128)S(1)}, f32[2,2560]{1,0:T(2,128)S(1)}, u32[]{:S(2)}, u32[]{:S(2)}) collective-permute-start(f32[2,2560]{1,0:T(2,128)S(1)} %slice.79), channel_id=1, source_target_pairs={{0,1},{1,2},{2,3},{3,4},{4,5},{5,6},{6,7},{7,8},{8,9},{9,10},{10,1... | collective-permute-start | bytes 61448 | tf_op jit(solution)/shard_map/ppermute | solution.py:35
  15.2 3.2 copy-start.35
  15.2 3.2 copy-start.37
  16.2 2.2 copy-start.23
  16.2 2.2 copy-start.25
  16.2 2.2 copy-start.27
  17.9 3.6 copy-start.8
  18.4 3.1 copy-start.10
  21.6 4.6 copy-start.33
  21.6 4.6 copy-start.32
  21.6 20.4 %all-to-all-start = ((f32[128,2,1280]{0,2,1:T(8,128)}), f32[128,2,1280]{0,2,1:T(8,128)S(1)}, u32[]{:S(2)}, u32[]{:S(2)}) async-start(f32[128,2,1280]{0,2,1:T(8,128)} %bitcast.267), calls=%async_computation | async-start | bytes 2621440 | tf_op jit(solution)/shard_map/all_to_all | solution.py:238
  25.3 125.8 %all-gather.7.cloned.1.call-start = ((), (), s32[]{:S(2)}) async-start(), calls=%async_computation.3 | async-start | bytes 10653696 | tf_op jit(solution)/shard_map/all_gather | solution.py:18
  25.5 75.7 %copy-start.31 = (s32[258]{0:T(512)}, s32[258]{0:T(512)S(1)}, u32[]{:S(2)}) copy-start(s32[258]{0:T(512)S(1)} %select_reduce_fusion) | copy-start | bytes 3100
  48.8 5.4 copy-start.12
  52.4 1.8 copy-start.39
  60.3 1.2 copy-start.22
  62.6 4.5 copy-start.44
  62.6 38.6 %all-to-all-start.1 = ((f32[128,2,1024]{2,0,1:T(8,128)}), f32[128,2,1024]{2,0,1:T(8,128)S(1)}, u32[]{:S(2)}, u32[]{:S(2)}) async-start(f32[128,2,1024]{2,0,1:T(8,128)} %bitcast.276), calls=%async_computation.1 | async-start | bytes 2097152 | tf_op jit(solution)/shard_map/all_to_all | solution.py:239
  66.4 298.9 %all-gather.9.cloned.1.call-start = ((), (), s32[]{:S(2)}) async-start(), calls=%async_computation.4 | async-start | bytes 10653696 | tf_op jit(solution)/shard_map/all_gather | solution.py:18
  103.6 1.9 copy-start.19
  235.0 2.3 copy-start.43
  235.0 2.3 slice-start
  238.5 2.1 copy-start
  240.6 1.1 copy-start.4
  246.4 2.0 copy-start.5
  251.1 1.5 copy-start.1
  255.8 2.1 copy-start
  257.9 1.1 copy-start.4
  263.7 1.9 copy-start.5
  268.4 1.5 copy-start.1
  271.8 3.2 copy-start.29
  272.0 3.0 copy-start.7
  275.0 1.8 copy-start.17
  278.0 2.6 copy-start.18
  278.0 2.6 copy-start.21
  471.8 2.2 copy-start.30
  483.5 2.1 copy-start.2
  485.6 3.6 copy-start.6
  488.0 1.2 copy-start.3
  507.4 2.1 copy-start.2
  509.5 3.6 copy-start.6
  511.9 1.2 copy-start.3
  521.7 4.5 copy-start.15
  521.7 4.5 copy-start.16
  523.9 2.3 copy-start.13
  524.0 2.3 copy-start.14
  524.0 2.3 copy-start.40
  528.1 12.0 %copy-start.34 = (s32[136]{0:T(256)S(1)}, s32[136]{0:T(256)}, u32[]{:S(2)}) copy-start(s32[136]{0:T(256)} %constant.226) | copy-start | bytes 1636
  565.6 1.4 copy-start.20
  569.7 23.5 %copy-start.36 = (f32[128]{0:T(128)S(1)}, f32[128]{0:T(128)}, u32[]{:S(2)}) copy-start(f32[128]{0:T(128)} %copy-done.35) | copy-start | bytes 1540
  569.7 23.5 %copy-start.38 = (f32[128]{0:T(128)S(1)}, f32[128]{0:T(128)}, u32[]{:S(2)}) copy-start(f32[128]{0:T(128)} %copy-done.37) | copy-start | bytes 1540
  572.2 21.0 %copy-start.9 = (f32[128,2560]{0,1:T(8,128)S(1)}, f32[128,2560]{0,1:T(8,128)}, u32[]{:S(2)}) copy-start(f32[128,2560]{0,1:T(8,128)} %copy-done.8) | copy-start | bytes 3932164
  572.2 21.0 %copy-start.11 = (f32[2,2560]{0,1:T(8,128)S(1)}, f32[2,2560]{0,1:T(8,128)}, u32[]{:S(2)}) copy-start(f32[2,2560]{0,1:T(8,128)} %copy-done.10) | copy-start | bytes 61444
  595.4 44.5 %copy-start.24 = (f32[2560]{0:T(1024)S(1)}, f32[2560]{0:T(1024)}, u32[]{:S(2)}) copy-start(f32[2560]{0:T(1024)} %copy-done.23) | copy-start | bytes 30724
  595.4 44.5 %copy-start.26 = (f32[2560]{0:T(1024)S(1)}, f32[2560]{0:T(1024)}, u32[]{:S(2)}) copy-start(f32[2560]{0:T(1024)} %copy-done.25) | copy-start | bytes 30724
  595.4 44.5 %copy-start.28 = (f32[2560]{0:T(1024)S(1)}, f32[2560]{0:T(1024)}, u32[]{:S(2)}) copy-start(f32[2560]{0:T(1024)} %copy-done.27) | copy-start | bytes 30724
  595.4 44.5 %copy-start.41 = (f32[128]{0:T(128)S(1)}, f32[128]{0:T(128)}, u32[]{:S(2)}) copy-start(f32[128]{0:T(128)} %get-tuple-element.1263) | copy-start | bytes 1540
  595.4 44.5 %copy-start.42 = (f32[128]{0:T(128)S(1)}, f32[128]{0:T(128)}, u32[]{:S(2)}) copy-start(f32[128]{0:T(128)} %get-tuple-element.1265) | copy-start | bytes 1540
  595.8 42.5 %collective-permute-start.1 = (f32[2,2560]{1,0:T(2,128)S(1)}, f32[2,2560]{1,0:T(2,128)S(1)}, u32[]{:S(2)}, u32[]{:S(2)}) collective-permute-start(f32[2,2560]{1,0:T(2,128)S(1)} %copy.278), channel_id=1, source_target_pairs={{1,0},{2,1},{3,2},{4,3},{5,4},{6,5},{7,6},{8,7},{9,8},{10,9},{11,1... | collective-permute-start | bytes 61448 | tf_op jit(solution)/shard_map/ppermute | solution.py:35
Sparse Core Ops, SparseCore 0:
  61.6 89.5 all-gather.6
  278.1 87.0 all-gather.8
where the time goes:
time: 663 us; the launch traced here: 653 us
  other arithmetic  183 us (28%)
  local copies, waits for them, and re-layouts  138 us (21%)
  blocking collectives  133 us (20%)
  waiting for transfers between devices  101 us (15%)
  matrix products  53.2 us (8%)
  between operations  15.8 us (2%)
  loops' own time  15 us (2%)
  starting transfers between devices  13.7 us (2%)
    select_n x64, other arithmetic, lap(): return jax.tree.map(lambda a, b: jnp.where(reached, a, b), new, before)  87.8 us
    all_gather x2, waiting for transfers between devices, carried_in(): everything = jax.tree.map(lambda part: lax.all_gather(part, axis), x)  85.5 us
    dynamic_slice x32, local copies, waits for them, and re-layouts, lap(): new = combine(before, jax.tree.map(lambda part: part[at], everything))  62.3 us
    psum x1, blocking collectives, on_device(): grad_conv = lax.psum(weight_part, ('seq', 'head'))  41.2 us
    all_gather x2, blocking collectives, carried_in(): everything = jax.tree.map(lambda part: lax.all_gather(part, axis), x)  38.4 us
    unnamed x1, blocking collectives  32.7 us
    sub x32, other arithmetic, combine(): carry_keep = 1.0 - following[2]  29.7 us
    all_to_all x1, blocking collectives, on_device(): lax.all_to_all(grad_mixed, 'head', split_axis=0, concat_axis=1, tiled=True)  21 us
  transfers between devices with their start and end apart: 6, of which 3 were waited for; matrix products, arithmetic and copies ran while one was open for 3% of the time, Pallas kernels for 0%

commit v1 on v0

v1 whole, which is shorter than its diff:
```python
import functools
import math

import jax
import jax.numpy as jnp
from jax import lax
from jax.experimental import pallas as pl
from jax.experimental.pallas import tpu as pltpu
from jax.sharding import PartitionSpec as P

KEY_DIM = 16
HEAD_DIM = 128
HEADS = 16
WIDTH = 2 * KEY_DIM + HEAD_DIM
MEMBERS = 8
FEATS = 160
BLOCK = 256
LANES = 128
MESH = pl.DeviceIdType.MESH
F32 = jnp.float32
BF16 = jnp.bfloat16


def halves(x):
    high = x.astype(BF16)
    return high, (x - high.astype(F32)).astype(BF16)


def dot(a, b, ca=1, cb=0):
    return lax.dot_general(a, b, (((ca,), (cb,)), ((), ())), preferred_element_type=F32)


def dot_halves(a, b, ca=1, cb=0):
    return dot(a[0], b[0], ca, cb) + (dot(a[0], b[1], ca, cb) + dot(a[1], b[0], ca, cb))


def features(x):
    twice = jnp.concatenate([x, x], axis=0)
    parts = [x * x * (1.0 / math.sqrt(2.0))]
    for d in range(1, 8):
        parts.append(x * twice[d : d + 16])
    parts.append(x[0:8] * x[8:16])
    parts.append(x)
    row = lax.broadcasted_iota(jnp.int32, (8, x.shape[1]), 0)
    parts.append((row == 0).astype(F32))
    return jnp.concatenate(parts, axis=0)


def features_pull(x, grad):
    twice = jnp.concatenate([x, x], axis=0)
    total = math.sqrt(2.0) * x * grad[0:16] + grad[136:152]
    for d in range(1, 8):
        g = grad[16 * d : 16 * d + 16]
        back = g * x
        back = jnp.concatenate([back, back], axis=0)[16 - d : 32 - d]
        total = total + g * twice[d : d + 16] + back
    g = grad[128:136]
    return total + jnp.concatenate([g * x[8:16], g * x[0:8]], axis=0)


def kernel(
    sub, side, groups, seq_name, head_name,
    docs_ref, p_ref, o_ref, wv_ref, wqk_ref,
    gp_ref, gw_ref,
    sv, sqk, v_buf, qk_buf, o_buf,
    bcol, brow, vm, qkm, qrow, kst, qf, kf,
    num, den, gn_buf, gd_buf,
    s_buf, n_buf, g_buf, gd_state, n_row, s_sum,
    dmv, dmqk, dvt, rv, rqk, wmsg, wtot,
    in_send, in_recv, halo_sem, state_send, state_recv,
    back_halo, out_send, out_recv, w_send, w_recv, wt_send, wt_recv,
):
    members = sub * side
    hpd = HEADS // members
    rows = p_ref.shape[0]
    tokens = rows * members
    total_len = tokens * groups
    ndoc = docs_ref.shape[0]
    seq = lax.axis_index(seq_name)
    group = seq // sub
    me = (seq % sub) * side + lax.axis_index(head_name)
    base = group * tokens

    def device(g, m):
        return (g * sub + m // side, m % side)

    def remote(src, dst, send, recv, target):
        return pltpu.make_async_remote_copy(
            src_ref=src, dst_ref=dst, send_sem=send, recv_sem=recv, device_id=target, device_id_type=MESH
        )

    barrier = pltpu.get_barrier_semaphore()

    def greet_member(r, _):
        pl.semaphore_signal(barrier, inc=1, device_id=device(group, (me + r) % members), device_id_type=MESH)
        return 0

    def greet_group(r, _):
        pl.semaphore_signal(barrier, inc=1, device_id=device((group + r) % groups, me), device_id_type=MESH)
        return 0

    lax.fori_loop(1, members, greet_member, 0)
    lax.fori_loop(1, groups, greet_group, 0)

    for n in range(HEADS):
        d, h = n // hpd, n % hpd
        first = WIDTH * n
        tile = (first // LANES) * LANES
        off = first - tile
        turned = p_ref[:, tile : tile + LANES].T
        sqk[d, 32 * h : 32 * h + 32, :] = turned[off : off + 32, :]
        sv[d, :, HEAD_DIM * h : HEAD_DIM * h + HEAD_DIM] = p_ref[:, first + 32 : first + WIDTH]

    pl.semaphore_wait(barrier, members - 1 + groups - 1)

    def in_copies(m, slot, target):
        at = pl.ds(pl.multiple_of(rows * slot, rows), rows)
        at_v = pl.ds(pl.multiple_of(rows * slot + 8, 8), rows)
        lanes = pl.ds(pl.multiple_of(m * hpd * HEAD_DIM, LANES), hpd * HEAD_DIM)
        return (
            remote(sqk.at[m], qk_buf.at[slot + 1], in_send.at[0, m], in_recv.at[0, slot], target),
            remote(sv.at[m], v_buf.at[at_v, :], in_send.at[1, m], in_recv.at[1, slot], target),
            remote(o_ref.at[:, lanes], o_buf.at[at, :], in_send.at[2, m], in_recv.at[2, slot], target),
        )

    def send_some(picked):
        def body(r, _):
            m = (me + r) % members
            copies = in_copies(m, me, device(group, m))
            for k in picked:
                copies[k].start()
            return 0

        lax.fori_loop(1, members, body, 0)

    def wait_some(picked):
        def body(r, _):
            m = (me + members - r) % members
            copies = in_copies(m, m, device(group, m))
            for k in picked:
                copies[k].wait_recv()
            return 0

        lax.fori_loop(1, members, body, 0)

    send_some((0, 1))
    send_some((2,))
    qk_buf[me + 1] = sqk[me]
    v_buf[pl.ds(pl.multiple_of(rows * me + 8, 8), rows), :] = sv[me]
    o_buf[pl.ds(pl.multiple_of(rows * me, rows), rows), :] = o_ref[
        :, pl.ds(pl.multiple_of(me * hpd * HEAD_DIM, LANES), hpd * HEAD_DIM)
    ]

    starts = []
    run = jnp.int32(0)
    for i in range(ndoc):
        starts.append(run)
        run = run + docs_ref[i]

    def begin_of(pos):
        out = jnp.zeros_like(pos)
        for s in starts:
            out = jnp.where(s <= pos, s, out)
        return out

    bcol[...] = begin_of(base + lax.broadcasted_iota(jnp.int32, (tokens, LANES), 0))
    pos_row = base + lax.broadcasted_iota(jnp.int32, (8, tokens), 1)
    brow[...] = begin_of(pos_row)
    my_first = begin_of(base)
    my_last = begin_of(base + tokens - 1)

    wait_some((0, 1))
    nxt, prv = (group + 1) % groups, (group + groups - 1) % groups
    halo = (
        remote(qk_buf.at[members], qk_buf.at[0], halo_sem.at[0], halo_sem.at[1], device(nxt, me)),
        remote(v_buf.at[pl.ds(tokens, 8), :], v_buf.at[pl.ds(0, 8), :], halo_sem.at[2], halo_sem.at[3], device(nxt, me)),
    )
    for c in halo:
        c.start()
    for c in halo:
        c.wait()

    pos = pos_row[0:1]
    beg = brow[0:1, :]
    off_row = pos - beg
    m1_row = (off_row >= 1).astype(F32)
    m2_row = (off_row >= 2).astype(F32)
    lead_row = (beg < base).astype(F32)
    tail_row = (beg == my_last).astype(F32)
    w_cols = [wqk_ref[:, j : j + 1] for j in range(3)]

    def qk_signal():
        sig = jnp.concatenate([qk_buf[m] for m in range(members + 1)], axis=1)
        return sig[:, LANES:], pltpu.roll(sig, 1, 1)[:, LANES:], pltpu.roll(sig, 2, 1)[:, LANES:]

    s0, s1, s2 = qk_signal()
    qkm[...] = (w_cols[0] * s0 + w_cols[1] * (s1 * m1_row) + w_cols[2] * (s2 * m2_row)) * (KEY_DIM ** (-0.25))

    def col_masks(t0, count):
        pcol = base + t0 + lax.broadcasted_iota(jnp.int32, (count, 1), 0)
        off = pcol - bcol[t0 : t0 + count, 0:1]
        return (off >= 1).astype(F32), (off >= 2).astype(F32)

    for b in range(tokens // BLOCK):
        t0 = b * BLOCK
        m1, m2 = col_masks(t0, BLOCK)
        a0 = v_buf[t0 + 8 : t0 + 8 + BLOCK, :]
        a1 = v_buf[t0 + 7 : t0 + 7 + BLOCK, :]
        a2 = v_buf[t0 + 6 : t0 + 6 + BLOCK, :]
        vm[t0 : t0 + BLOCK, :] = wv_ref[0:1, :] * a0 + wv_ref[1:2, :] * (a1 * m1) + wv_ref[2:3, :] * (a2 * m2)

    def head_lanes(h):
        return pl.ds(pl.multiple_of(h * HEAD_DIM, LANES), HEAD_DIM)

    def q_of(h):
        return qkm[pl.ds(pl.multiple_of(32 * h, 8), 16), :]

    def k_of(h):
        return qkm[pl.ds(pl.multiple_of(32 * h + 16, 8), 16), :]

    def key_state(h, _):
        k = k_of(h)
        kh, kl = halves(k)
        kst[h] = jnp.concatenate([kh, kl, kh, kl], axis=0)
        feat = halves(features(k) * tail_row)
        kf[h, 0], kf[h, 1] = feat
        s_buf[group, h] = dot_halves(feat, halves(vm[:, head_lanes(h)]))
        ones = jnp.ones((8, tokens), BF16)
        norm = dot(ones, feat[0], 1, 1) + dot(ones, feat[1], 1, 1)
        n_buf[group, h] = jnp.concatenate([norm, jnp.zeros((8, 256 - FEATS), F32)], axis=1)
        return 0

    lax.fori_loop(0, hpd, key_state, 0)

    def state_copies(big, small, kind, slot, g):
        target = device(g, me)
        return (
            remote(big.at[slot], big.at[slot], state_send.at[kind, 0, g], state_recv.at[kind, 0, slot], target),
            remote(small.at[slot], small.at[slot], state_send.at[kind, 1, g], state_recv.at[kind, 1, slot], target),
        )

    def send_states(big, small, kind):
        def body(r, _):
            for c in state_copies(big, small, kind, group, (group + r) % groups):
                c.start()
            return 0

        lax.fori_loop(1, groups, body, 0)

    def wait_states(big, small, kind):
        def body(r, _):
            g = (group + groups - r) % groups
            for c in state_copies(big, small, kind, g, g):
                c.wait_recv()
            return 0

        lax.fori_loop(1, groups, body, 0)

    send_states(s_buf, n_buf, 0)

    def scores(h, i):
        wide = (i + 1) * BLOCK
        t0 = i * BLOCK
        u = 1.0 + dot(qrow[h, t0 : t0 + BLOCK, :], kst[h, :, 0:wide])
        s_pos = lax.broadcasted_iota(jnp.int32, (BLOCK, wide), 1)
        t_pos = t0 + lax.broadcasted_iota(jnp.int32, (BLOCK, wide), 0)
        begin = bcol[t0 : t0 + BLOCK, 0:1] - base
        allowed = (s_pos >= begin) & (s_pos <= t_pos)
        return allowed, u, jnp.where(allowed, 0.5 + 0.5 * (u * u), 0.0)

    def forward(h, _):
        q = q_of(h)
        qh, ql = halves(q)
        qh, ql = qh.astype(F32), ql.astype(F32)
        qrow[h] = jnp.concatenate([qh, qh, ql, ql], axis=0).T.astype(BF16)
        qf[h, 0], qf[h, 1] = halves(features(q) * lead_row)
        vh, vl = halves(vm[:, head_lanes(h)])
        both = jnp.concatenate([vh, vl], axis=1)
        for i in range(tokens // BLOCK):
            t0, wide = i * BLOCK, (i + 1) * BLOCK
            _, _, sc = scores(h, i)
            sh, sl = halves(sc)
            wide_num = dot(sh, both[0:wide])
            num[h, t0 : t0 + BLOCK, :] = wide_num[:, 0:128] + (wide_num[:, 128:256] + dot(sl, vh[0:wide]))
            den[h, t0 : t0 + BLOCK, :] = jnp.broadcast_to(jnp.sum(sc, axis=1, keepdims=True), (BLOCK, LANES))
        return 0

    lax.fori_loop(0, hpd, forward, 0)
    wait_some((2,))
    wait_states(s_buf, n_buf, 0)

    s_sum[...] = jnp.zeros_like(s_sum)
    n_row[...] = jnp.zeros_like(n_row)

    def add_earlier(g, _):
        last = begin_of(g * tokens + tokens - 1)
        weight = ((g < group) & (last == my_first)).astype(F32)
        s_sum[...] = s_sum[...] + weight * s_buf[g]
        n_row[...] = n_row[...] + weight * n_buf[g]
        return 0

    lax.fori_loop(0, groups, add_earlier, 0)

    def normalise(h, _):
        norm = jnp.broadcast_to(n_row[h, 0:1, 0:FEATS], (HEAD_DIM, FEATS))
        left = halves(jnp.concatenate([s_sum[h].T, norm], axis=0))
        for i in range(tokens // BLOCK):
            t0 = i * BLOCK
            carried = dot_halves(left, (qf[h, 0, :, t0 : t0 + BLOCK], qf[h, 1, :, t0 : t0 + BLOCK])).T
            n_all = num[h, t0 : t0 + BLOCK, :] + carried[:, 0:128]
            inv = 1.0 / (den[h, t0 : t0 + BLOCK, :] + carried[:, 128:256])
            gn = o_buf[t0 : t0 + BLOCK, head_lanes(h)] * inv
            gn_buf[h, t0 : t0 + BLOCK, :] = gn
            gd = -jnp.sum(gn * (n_all * inv), axis=1, keepdims=True)
            gd_buf[h, t0 : t0 + BLOCK, :] = jnp.broadcast_to(gd, (BLOCK, LANES))
        feat = (qf[h, 0], qf[h, 1])
        g_buf[group, h] = dot_halves(feat, halves(gn_buf[h]))
        gd_t = gd_buf[h].T[0:8]
        norm = dot_halves(halves(gd_t), feat, 1, 1)
        gd_state[group, h] = jnp.concatenate([norm, jnp.zeros((8, 256 - FEATS), F32)], axis=1)
        return 0

    lax.fori_loop(0, hpd, normalise, 0)
    send_states(g_buf, gd_state, 1)

    def column(row):
        return jnp.broadcast_to(row, (LANES, 256)).T[0:FEATS, 0:1]

    def backward(h, _):
        vh, vl = halves(vm[:, head_lanes(h)])
        v_twice = jnp.concatenate([vh, vh], axis=1)
        qh, ql = halves(q_of(h))
        kh, kl = halves(k_of(h))
        q_both = jnp.concatenate([qh, ql], axis=0)
        k_both = jnp.concatenate([kh, kl], axis=0)
        dvt[h] = jnp.zeros((HEAD_DIM, tokens), F32)
        at_q = pl.ds(pl.multiple_of(32 * h, 8), 16)
        at_k = pl.ds(pl.multiple_of(32 * h + 16, 8), 16)
        dmqk[at_k, 0:tokens] = jnp.zeros((16, tokens), F32)
        for i in range(tokens // BLOCK):
            t0, wide = i * BLOCK, (i + 1) * BLOCK
            allowed, u, sc = scores(h, i)
            gn = gn_buf[h, t0 : t0 + BLOCK, :]
            gh, gl = halves(gn)
            ds = dot(jnp.concatenate([gh, gl], axis=1), v_twice[0:wide], 1, 1) + dot(gh, vl[0:wide], 1, 1)
            dx = jnp.where(allowed, (ds + gd_buf[h, t0 : t0 + BLOCK, 0:1]) * u, 0.0)
            dh, dl = halves(dx)
            sh, sl = halves(sc)
            gth, gtl = halves(gn.T)
            dv = dot(jnp.concatenate([gth, gtl], axis=0), sh)
            dvt[h, :, 0:wide] += dv[0:128] + (dv[128:256] + dot(gth, sl))
            dk = dot(q_both[:, t0 : t0 + BLOCK], dh)
            dmqk[at_k, 0:wide] += dk[0:16] + (dk[16:32] + dot(qh[:, t0 : t0 + BLOCK], dl))
            dq = dot(k_both[:, 0:wide], dh, 1, 1)
            dmqk[at_q, t0 : t0 + BLOCK] = dq[0:16] + (dq[16:32] + dot(kh[:, 0:wide], dl, 1, 1))
        gd_row = gd_buf[h].T[0:1]
        dqf = dot_halves(halves(s_sum[h]), halves(gn_buf[h]), 1, 1) + column(n_row[h, 0:1, :]) * gd_row
        dmqk[at_q, 0:tokens] += features_pull(q_of(h), dqf * lead_row)
        return 0

    lax.fori_loop(0, hpd, backward, 0)
    wait_states(g_buf, gd_state, 1)

    s_sum[...] = jnp.zeros_like(s_sum)
    n_row[...] = jnp.zeros_like(n_row)

    def add_later(g, _):
        first = begin_of(g * tokens)
        weight = ((g > group) & (first == my_last)).astype(F32)
        s_sum[...] = s_sum[...] + weight * g_buf[g]
        n_row[...] = n_row[...] + weight * gd_state[g]
        return 0

    lax.fori_loop(0, groups, add_later, 0)

    def finish(h, _):
        at_k = pl.ds(pl.multiple_of(32 * h + 16, 8), 16)
        dkf = dot_halves(halves(s_sum[h]), halves(vm[:, head_lanes(h)]), 1, 1) + column(n_row[h, 0:1, :])
        dmqk[at_k, 0:tokens] += features_pull(k_of(h), dkf * tail_row)
        dv = dvt[h] + dot_halves(halves(s_sum[h].T), (kf[h, 0], kf[h, 1]))
        dmv[0:tokens, head_lanes(h)] = dv.T
        return 0

    lax.fori_loop(0, hpd, finish, 0)
    dmqk[:, 0:tokens] = dmqk[:, 0:tokens] * (KEY_DIM ** (-0.25))

    def drain_in(r, _):
        m = (me + r) % members
        for c in in_copies(m, me, device(group, m)):
            c.wait_send()
        return 0

    lax.fori_loop(1, members, drain_in, 0)

    late = (
        remote(dmqk.at[:, pl.ds(0, LANES)], dmqk.at[:, pl.ds(tokens, LANES)], back_halo.at[0], back_halo.at[1], device(prv, me)),
        remote(dmv.at[pl.ds(0, 8), :], dmv.at[pl.ds(tokens, 8), :], back_halo.at[2], back_halo.at[3], device(prv, me)),
    )
    for c in late:
        c.start()
    for c in late:
        c.wait()

    far = tokens + LANES
    pos_far = base + lax.broadcasted_iota(jnp.int32, (1, far), 1)
    inside = pos_far < total_len
    off_far = pos_far - begin_of(pos_far)
    dm = dmqk[...]
    dm1 = jnp.where(inside & (off_far >= 1), dm, 0.0)
    dm2 = jnp.where(inside & (off_far >= 2), dm, 0.0)
    back = (
        w_cols[0] * dm[:, 0:tokens]
        + w_cols[1] * pltpu.roll(dm1, far - 1, 1)[:, 0:tokens]
        + w_cols[2] * pltpu.roll(dm2, far - 2, 1)[:, 0:tokens]
    )
    for m in range(members):
        sqk[m] = back[:, m * rows : m * rows + rows]
    s0, s1, s2 = qk_signal()
    taps = [
        jnp.sum(dm[:, 0:tokens] * s0, axis=1, keepdims=True),
        jnp.sum(dm1[:, 0:tokens] * s1, axis=1, keepdims=True),
        jnp.sum(dm2[:, 0:tokens] * s2, axis=1, keepdims=True),
    ]
    lane = lax.broadcasted_iota(jnp.int32, (LANES, LANES), 1)
    square = jnp.zeros((LANES, LANES), F32)
    for j in range(3):
        tall = jnp.concatenate([taps[j], jnp.zeros((LANES - taps[j].shape[0], 1), F32)], axis=0)
        square = jnp.where(lane == j, tall, square)
    wmsg[group, :, hpd * HEAD_DIM :] = square.T[0:8]

    sums = [jnp.zeros((1, hpd * HEAD_DIM), F32) for _ in range(3)]
    for m in range(members):
        t0 = m * rows
        count = rows + 8
        pcol = base + t0 + lax.broadcasted_iota(jnp.int32, (count, 1), 0)
        off = pcol - begin_of(pcol)
        ok = pcol < total_len
        d0 = dmv[t0 : t0 + count, :]
        d1 = jnp.where(ok & (off >= 1), d0, 0.0)
        d2 = jnp.where(ok & (off >= 2), d0, 0.0)
        sv[m] = wv_ref[0:1, :] * d0[0:rows] + wv_ref[1:2, :] * d1[1 : rows + 1] + wv_ref[2:3, :] * d2[2 : rows + 2]
        a0 = v_buf[t0 + 8 : t0 + 8 + rows, :]
        a1 = v_buf[t0 + 7 : t0 + 7 + rows, :]
        a2 = v_buf[t0 + 6 : t0 + 6 + rows, :]
        for j, (d, a) in enumerate(((d0, a0), (d1, a1), (d2, a2))):
            sums[j] = sums[j] + jnp.sum(d[0:rows] * a, axis=0, keepdims=True)
    wmsg[group, :, 0 : hpd * HEAD_DIM] = jnp.concatenate(sums + [jnp.zeros((5, hpd * HEAD_DIM), F32)], axis=0)

    def w_copy(slot, g):
        return remote(wmsg.at[slot], wmsg.at[slot], w_send.at[g], w_recv.at[slot], device(g, me))

    def send_w(r, _):
        w_copy(group, (group + r) % groups).start()
        return 0

    lax.fori_loop(1, groups, send_w, 0)

    def out_copies(m, slot):
        target = device(group, m)
        return (
            remote(sqk.at[m], rqk.at[slot], out_send.at[0, m], out_recv.at[0, slot], target),
            remote(sv.at[m], rv.at[slot], out_send.at[1, m], out_recv.at[1, slot], target),
        )

    def send_out(r, _):
        for c in out_copies((me + r) % members, me):
            c.start()
        return 0

    lax.fori_loop(1, members, send_out, 0)
    rqk[me] = sqk[me]
    rv[me] = sv[me]

    def wait_w(r, _):
        g = (group + groups - r) % groups
        w_copy(g, g).wait_recv()
        return 0

    lax.fori_loop(1, groups, wait_w, 0)
    wtot[me] = lax.fori_loop(0, groups, lambda g, acc: acc + wmsg[g], jnp.zeros(wmsg.shape[1:], F32))

    def send_t(r, _):
        m = (me + r) % members
        remote(wtot.at[me], wtot.at[me], wt_send.at[m], wt_recv.at[me], device(group, m)).start()
        return 0

    lax.fori_loop(1, members, send_t, 0)

    def wait_out(r, _):
        m = (me + members - r) % members
        for c in out_copies(m, m):
            c.wait_recv()
        remote(wtot.at[m], wtot.at[m], wt_send.at[m], wt_recv.at[m], device(group, m)).wait_recv()
        return 0

    lax.fori_loop(1, members, wait_out, 0)

    for n in range(HEADS):
        d, h = n // hpd, n % hpd
        first = WIDTH * n
        tall = jnp.concatenate([rqk[d, 32 * h : 32 * h + 32, :], jnp.zeros((96, rows), F32)], axis=0)
        gp_ref[:, first : first + 32] = tall.T[:, 0:32]
        gp_ref[:, first + 32 : first + WIDTH] = rv[d, :, HEAD_DIM * h : HEAD_DIM * h + HEAD_DIM]
        gw_ref[:, first : first + 32] = wtot[d, 0:3, hpd * HEAD_DIM + 32 * h : hpd * HEAD_DIM + 32 * h + 32]
        gw_ref[:, first + 32 : first + WIDTH] = wtot[d, 0:3, HEAD_DIM * h : HEAD_DIM * h + HEAD_DIM]

    def drain_members(r, _):
        m = (me + r) % members
        for c in out_copies(m, me):
            c.wait_send()
        remote(wtot.at[me], wtot.at[me], wt_send.at[m], wt_recv.at[me], device(group, m)).wait_send()
        return 0

    lax.fori_loop(1, members, drain_members, 0)

    def drain_groups(r, _):
        g = (group + r) % groups
        for c in state_copies(s_buf, n_buf, 0, group, g) + state_copies(g_buf, gd_state, 1, group, g):
            c.wait_send()
        w_copy(group, g).wait_send()
        return 0

    lax.fori_loop(1, groups, drain_groups, 0)


def on_device(sub, side, groups, projected, out_grads, conv_weight, doc_lengths):
    members = sub * side
    hpd = HEADS // members
    rows = projected.shape[0]
    tokens = rows * members
    me = (lax.axis_index("seq") % sub) * side + lax.axis_index("head")
    mine = lax.dynamic_slice_in_dim(conv_weight, me * hpd * WIDTH, hpd * WIDTH, 1).reshape(3, hpd, WIDTH)
    wqk = mine[:, :, 0:32].reshape(3, hpd * 32).T
    wv = mine[:, :, 32:].reshape(3, hpd * HEAD_DIM)
    wide = hpd * HEAD_DIM
    vmem = pltpu.VMEM
    dma = pltpu.SemaphoreType.DMA
    scratch = [
        vmem((members, rows, wide), F32),
        vmem((members, hpd * 32, rows), F32),
        vmem((tokens + 8, wide), F32),
        vmem((members + 1, hpd * 32, rows), F32),
        vmem((tokens, wide), F32),
        vmem((tokens, LANES), jnp.int32),
        vmem((8, tokens), jnp.int32),
        vmem((tokens, wide), F32),
        vmem((hpd * 32, tokens), F32),
        vmem((hpd, tokens, 64), BF16),
        vmem((hpd, 64, tokens), BF16),
        vmem((hpd, 2, FEATS, tokens), BF16),
        vmem((hpd, 2, FEATS, tokens), BF16),
        vmem((hpd, tokens, LANES), F32),
        vmem((hpd, tokens, LANES), F32),
        vmem((hpd, tokens, LANES), F32),
        vmem((hpd, tokens, LANES), F32),
        vmem((groups, hpd, FEATS, HEAD_DIM), F32),
        vmem((groups, hpd, 8, 256), F32),
        vmem((groups, hpd, FEATS, HEAD_DIM), F32),
        vmem((groups, hpd, 8, 256), F32),
        vmem((hpd, 8, 256), F32),
        vmem((hpd, FEATS, HEAD_DIM), F32),
        vmem((tokens + 8, wide), F32),
        vmem((hpd * 32, tokens + LANES), F32),
        vmem((hpd, HEAD_DIM, tokens), F32),
        vmem((members, rows, wide), F32),
        vmem((members, hpd * 32, rows), F32),
        vmem((groups, 8, wide + LANES), F32),
        vmem((members, 8, wide + LANES), F32),
        dma((3, members)),
        dma((3, members)),
        dma((4,)),
        dma((2, 2, groups)),
        dma((2, 2, groups)),
        dma((4,)),
        dma((2, members)),
        dma((2, members)),
        dma((groups,)),
        dma((groups,)),
        dma((members,)),
        dma((members,)),
    ]
    spec = pl.BlockSpec(memory_space=pltpu.VMEM)
    return pl.pallas_call(
        functools.partial(kernel, sub, side, groups, "seq", "head"),
        out_shape=(
            jax.ShapeDtypeStruct(projected.shape, F32),
            jax.ShapeDtypeStruct(conv_weight.shape, F32),
        ),
        in_specs=[pl.BlockSpec(memory_space=pltpu.SMEM), spec, spec, spec, spec],
        out_specs=(spec, spec),
        scratch_shapes=scratch,
        compiler_params=pltpu.CompilerParams(
            collective_id=0, has_side_effects=True, vmem_limit_bytes=60 * 1024 * 1024
        ),
        name="layer_backward",
    )(doc_lengths, projected, out_grads, wv, wqk)


def solution(mesh):
    side = mesh.shape["head"]
    sub = max(1, MEMBERS // side)
    groups = mesh.shape["seq"] // sub
    return jax.shard_map(
        functools.partial(on_device, sub, side, groups),
        mesh=mesh,
        in_specs=(P(("seq", "head"), None), P(("seq", "head"), None), P(), P()),
        out_specs=(P(("seq", "head"), None), P()),
        check_vma=False,
    )
```

time: 663 us -> 96.5 us (0.15)
  the two profiles are of different devices: /device:TPU:0 before, /device:TPU:21 now
where the time goes in v1:
time: 96.5 us; the launch traced here: 96.3 us
  Pallas kernels  90.2 us (93%)
  local copies, waits for them, and re-layouts  5.4 us (6%)
    pallas_call x1, Pallas kernels, on_device(): pl.pallas_call(functools.partial(kernel, sub, side, groups, 'seq', 'head'...  90.2 us
    unnamed x8, local copies, waits for them, and re-layouts  4.53 us

profile of v1, /device:TPU:21, one launch (start us, length us, event | category | flops | bytes accessed | tf_op | source)
XLA Modules:
  0.0 96.3 jit_solution(10452358782496520694)
XLA Ops:
  0.6 0.0 copy-start
  0.7 0.8 copy-done
  1.4 0.1 constant_dynamic-slice_fusion
  1.5 0.1 reshape.13
  1.6 0.1 slice_bitcast_fusion
  1.7 0.6 copy.10
  2.3 0.7 copy.7
  3.0 90.2 %layer_backward.1 = (f32[128,2560]{1,0:T(8,128)}, f32[3,2560]{1,0:T(4,128)}) custom-call(s32[4]{0:T(128)} %docs_ref.1, f32[128,2560]{1,0:T(8,128)} %p_ref.1, f32[128,2048]{1,0:T(8,128)} %o_ref.1, f32[3,256]{1,0:T(4,128)} %bitcast.9, f32[64,3]{1,0:T(8,128)} %bitcast.8), custom_call_target="tpu_custom_call" | custom-call | tf_op jit(solution)/shard_map/layer_backward/pallas_call | solution.py:583
  93.2 0.0 copy-start.1
  93.2 2.5 %copy.13 = f32[128,2560]{1,0:T(8,128)} copy(f32[128,2560]{1,0:T(8,128)} %get-tuple-element.4) | data formatting | bytes 2621440
  95.7 0.0 copy-done.1
  95.7 0.6 copy.14
  (1 shorter events, 0.0 us)
Async XLA Ops:
  0.6 0.8 copy-start
  93.2 2.5 %copy-start.1 = (f32[3,2560]{1,0:T(4,128)S(1)}, f32[3,2560]{1,0:T(4,128)}, u32[]{:S(2)}) copy-start(f32[3,2560]{1,0:T(4,128)} %get-tuple-element.5) | copy-start | bytes 92164

commit v2 on v1

v2 whole, which is shorter than its diff:
```python
import functools
import math

import jax
import jax.numpy as jnp
from jax import lax
from jax.experimental import pallas as pl
from jax.experimental.pallas import tpu as pltpu
from jax.sharding import PartitionSpec as P

KEY_DIM = 16
HEAD_DIM = 128
HEADS = 16
WIDTH = 2 * KEY_DIM + HEAD_DIM
MEMBERS = 8
FEATS = 160
BLOCK = 256
LANES = 128
MESH = pl.DeviceIdType.MESH
F32 = jnp.float32
BF16 = jnp.bfloat16


def halves(x):
    high = x.astype(BF16)
    return high, (x - high.astype(F32)).astype(BF16)


def dot(a, b, ca=1, cb=0):
    return lax.dot_general(a, b, (((ca,), (cb,)), ((), ())), preferred_element_type=F32)


def dot_halves(a, b, ca=1, cb=0):
    return dot(a[0], b[0], ca, cb) + (dot(a[0], b[1], ca, cb) + dot(a[1], b[0], ca, cb))


def features(x):
    twice = jnp.concatenate([x, x], axis=0)
    parts = [x * x * (1.0 / math.sqrt(2.0))]
    for d in range(1, 8):
        parts.append(x * twice[d : d + 16])
    parts.append(x[0:8] * x[8:16])
    parts.append(x)
    row = lax.broadcasted_iota(jnp.int32, (8, x.shape[1]), 0)
    parts.append((row == 0).astype(F32))
    return jnp.concatenate(parts, axis=0)


def features_pull(x, grad):
    twice = jnp.concatenate([x, x], axis=0)
    total = math.sqrt(2.0) * x * grad[0:16] + grad[136:152]
    for d in range(1, 8):
        g = grad[16 * d : 16 * d + 16]
        back = g * x
        back = jnp.concatenate([back, back], axis=0)[16 - d : 32 - d]
        total = total + g * twice[d : d + 16] + back
    g = grad[128:136]
    return total + jnp.concatenate([g * x[8:16], g * x[0:8]], axis=0)


def kernel(
    sub, side, groups, reach, seq_name, head_name,
    docs_ref, p_ref, o_ref, w_ref,
    gp_ref, gw_ref,
    sv, sqk, v_buf, qk_buf, o_buf, wv_all, wqk_all,
    bcol, brow, vm, qkm, qrow, kst, qf, kf,
    num, den, gn_buf, gd_buf,
    s_buf, n_buf, g_buf, gd_state, n_row, s_sum,
    dmv, dmqk, dvt, rv, rqk, wmsg, wtot,
    in_send, in_recv, halo_send, halo_recv, state_send, state_recv,
    back_send, back_recv, out_send, out_recv, w_send, w_recv, wt_send, wt_recv,
):
    members = sub * side
    hpd = HEADS // members
    rows = p_ref.shape[0]
    tokens = rows * members
    total_len = tokens * groups
    ndoc = docs_ref.shape[0]
    seq = lax.axis_index(seq_name)
    group = seq // sub
    me = (seq % sub) * side + lax.axis_index(head_name)
    base = group * tokens
    nxt, prv = (group + 1) % groups, (group + groups - 1) % groups
    is_last = me == members - 1

    def device(g, m):
        return (g * sub + m // side, m % side)

    def remote(src, dst, send, recv, target):
        return pltpu.make_async_remote_copy(
            src_ref=src, dst_ref=dst, send_sem=send, recv_sem=recv, device_id=target, device_id_type=MESH
        )

    def loop(low, high, body):
        def step(r, _):
            body(r)
            return 0

        lax.fori_loop(low, high, step, 0)

    barrier = pltpu.get_barrier_semaphore()

    def greet(target):
        pl.semaphore_signal(barrier, inc=1, device_id=target, device_id_type=MESH)

    loop(1, members, lambda r: greet(device(group, (me + r) % members)))
    loop(1, groups, lambda r: greet(device((group + r) % groups, me)))

    @pl.when(is_last)
    def _():
        loop(0, members - 1, lambda m: greet(device(nxt, m)))

    @pl.when(jnp.logical_not(is_last))
    def _():
        greet(device(prv, members - 1))

    for n in range(HEADS):
        d, h = n // hpd, n % hpd
        first = WIDTH * n
        tile = (first // LANES) * LANES
        off = first - tile
        turned = p_ref[:, tile : tile + LANES].T
        sqk[d, h] = turned[off : off + 32, :]
        sv[d, h] = p_ref[:, first + 32 : first + WIDTH]

    pl.semaphore_wait(barrier, members - 1 + groups - 1 + jnp.where(is_last, members - 1, 1))

    def qk_copy(h, m, slot):
        return remote(
            sqk.at[m, h], qk_buf.at[slot + 1, h], in_send.at[0, h, m], in_recv.at[0, h, slot], device(group, m)
        )

    def v_copy(h, m, slot):
        at = pl.ds(pl.multiple_of(rows * slot + 8, 8), rows)
        return remote(
            sv.at[m, h], v_buf.at[h, at, :], in_send.at[1, h, m], in_recv.at[1, h, slot], device(group, m)
        )

    def o_lanes(h, m):
        return pl.ds(pl.multiple_of((m * hpd + h) * HEAD_DIM, LANES), HEAD_DIM)

    def o_copy(h, m, slot):
        at = pl.ds(pl.multiple_of(rows * slot, rows), rows)
        return remote(
            o_ref.at[:, o_lanes(h, m)], o_buf.at[h, at, :], in_send.at[2, h, m], in_recv.at[2, h, slot],
            device(group, m),
        )

    def halo_qk(h, m, to):
        return remote(sqk.at[m, h], qk_buf.at[0, h], halo_send.at[0, h, m], halo_recv.at[0, h], device(to, m))

    def halo_v(h, m, to):
        return remote(
            sv.at[m, h, pl.ds(rows - 8, 8), :], v_buf.at[h, pl.ds(0, 8), :],
            halo_send.at[1, h, m], halo_recv.at[1, h], device(to, m),
        )

    def send_in(h):
        @pl.when(is_last)
        def _():
            def one(m):
                halo_qk(h, m, nxt).start()
                halo_v(h, m, nxt).start()

            loop(0, members, one)

        def one(r):
            m = (me + r) % members
            qk_copy(h, m, me).start()
            v_copy(h, m, me).start()

        loop(1, members, one)

    loop(0, hpd, send_in)
    loop(0, hpd, lambda h: loop(1, members, lambda r: o_copy(h, (me + r) % members, me).start()))

    def keep_own(h):
        qk_buf[me + 1, h] = sqk[me, h]
        v_buf[h, pl.ds(pl.multiple_of(rows * me + 8, 8), rows), :] = sv[me, h]
        o_buf[h, pl.ds(pl.multiple_of(rows * me, rows), rows), :] = o_ref[:, o_lanes(h, me)]

    loop(0, hpd, keep_own)

    for n in range(HEADS):
        d, h = n // hpd, n % hpd
        first = WIDTH * n
        tile = (first // LANES) * LANES
        off = first - tile
        square = jnp.concatenate([w_ref[:, tile : tile + LANES], jnp.zeros((LANES - 3, LANES), F32)], axis=0)
        wqk_all[d, h] = square.T[off : off + 32, :]
        wv_all[d, h, 0:3, :] = w_ref[:, first + 32 : first + WIDTH]

    starts = []
    run = jnp.int32(0)
    for i in range(ndoc):
        starts.append(run)
        run = run + docs_ref[i]

    def begin_of(pos):
        out = jnp.zeros_like(pos)
        for s in starts:
            out = jnp.where(s <= pos, s, out)
        return out

    bcol[...] = begin_of(base + lax.broadcasted_iota(jnp.int32, (tokens, LANES), 0))
    pos_row = base + lax.broadcasted_iota(jnp.int32, (8, tokens), 1)
    brow[...] = begin_of(pos_row)
    my_first = begin_of(base)
    my_last = begin_of(base + tokens - 1)

    pos = pos_row[0:1]
    beg = brow[0:1, :]
    off_row = pos - beg
    m1_row = (off_row >= 1).astype(F32)
    m2_row = (off_row >= 2).astype(F32)
    lead_row = (beg < base).astype(F32)
    tail_row = (beg == my_last).astype(F32)

    def qk_signal(h):
        sig = jnp.concatenate([qk_buf[m, h] for m in range(members + 1)], axis=1)
        return sig[:, LANES:], pltpu.roll(sig, 1, 1)[:, LANES:], pltpu.roll(sig, 2, 1)[:, LANES:]

    def taps_of(h):
        return [wqk_all[me, h, :, j : j + 1] for j in range(3)], [wv_all[me, h, j : j + 1, :] for j in range(3)]

    def q_of(h):
        return qkm[h, 0:16, :]

    def k_of(h):
        return qkm[h, 16:32, :]

    def state_copy(refs, kind, part, h, r):
        g = group + r if kind == 0 else group - r
        ref = refs[part]
        return remote(
            ref.at[0, h], ref.at[r, h], state_send.at[kind, part, h, r], state_recv.at[kind, part, h, r], device(g, me)
        )

    def ahead(kind, r):
        return group + r < groups if kind == 0 else group >= r

    def each_state(kind, to, body):
        def one(r):
            @pl.when(ahead(kind, r) if to else ahead(1 - kind, r))
            def _():
                body(r)

        loop(1, reach + 1, one)

    keys = (s_buf, n_buf)
    grads = (g_buf, gd_state)

    def arrive(h):
        def one(r):
            m = (me + members - r) % members
            qk_copy(h, m, m).wait_recv()
            v_copy(h, m, m).wait_recv()

        loop(1, members, one)
        halo_qk(h, me, prv).wait_recv()
        halo_v(h, me, prv).wait_recv()
        w_cols, w_rows = taps_of(h)
        s0, s1, s2 = qk_signal(h)
        qkm[h] = (w_cols[0] * s0 + w_cols[1] * (s1 * m1_row) + w_cols[2] * (s2 * m2_row)) * (KEY_DIM ** (-0.25))
        for b in range(tokens // BLOCK):
            t0 = b * BLOCK
            off = base + t0 + lax.broadcasted_iota(jnp.int32, (BLOCK, LANES), 0) - bcol[t0 : t0 + BLOCK, :]
            a0 = v_buf[h, t0 + 8 : t0 + 8 + BLOCK, :]
            a1 = jnp.where(off >= 1, v_buf[h, t0 + 7 : t0 + 7 + BLOCK, :], 0.0)
            a2 = jnp.where(off >= 2, v_buf[h, t0 + 6 : t0 + 6 + BLOCK, :], 0.0)
            vm[h, t0 : t0 + BLOCK, :] = w_rows[0] * a0 + w_rows[1] * a1 + w_rows[2] * a2
        k = k_of(h)
        kh, kl = halves(k)
        kst[h] = jnp.concatenate([kh, kl, kh, kl], axis=0)
        feat = halves(features(k) * tail_row)
        kf[h, 0], kf[h, 1] = feat
        ones = jnp.ones((8, tokens), BF16)
        norm = dot(ones, feat[0], 1, 1) + dot(ones, feat[1], 1, 1)
        n_buf[0, h] = jnp.concatenate([norm, jnp.zeros((8, 256 - FEATS), F32)], axis=1)
        each_state(0, True, lambda r: state_copy(keys, 0, 1, h, r).start())
        s_buf[0, h] = dot_halves(feat, halves(vm[h]))
        each_state(0, True, lambda r: state_copy(keys, 0, 0, h, r).start())

    loop(0, hpd, arrive)

    def scores(h, i):
        wide = (i + 1) * BLOCK
        t0 = i * BLOCK
        u = 1.0 + dot(qrow[h, t0 : t0 + BLOCK, :], kst[h, :, 0:wide])
        s_pos = lax.broadcasted_iota(jnp.int32, (BLOCK, wide), 1)
        t_pos = t0 + lax.broadcasted_iota(jnp.int32, (BLOCK, wide), 0)
        begin = bcol[t0 : t0 + BLOCK, 0:1] - base
        allowed = (s_pos >= begin) & (s_pos <= t_pos)
        return allowed, u, jnp.where(allowed, 0.5 + 0.5 * (u * u), 0.0)

    def forward(h):
        q = q_of(h)
        qh, ql = halves(q)
        qh, ql = qh.astype(F32), ql.astype(F32)
        qrow[h] = jnp.concatenate([qh, qh, ql, ql], axis=0).T.astype(BF16)
        qf[h, 0], qf[h, 1] = halves(features(q) * lead_row)
        vh, vl = halves(vm[h])
        both = jnp.concatenate([vh, vl], axis=1)
        for i in range(tokens // BLOCK):
            t0, wide = i * BLOCK, (i + 1) * BLOCK
            _, _, sc = scores(h, i)
            sh, sl = halves(sc)
            wide_num = dot(sh, both[0:wide])
            num[h, t0 : t0 + BLOCK, :] = wide_num[:, 0:128] + (wide_num[:, 128:256] + dot(sl, vh[0:wide]))
            den[h, t0 : t0 + BLOCK, :] = jnp.broadcast_to(jnp.sum(sc, axis=1, keepdims=True), (BLOCK, LANES))

    loop(0, hpd, forward)

    def gather(kind, part, refs, total, h):
        total[h] = jnp.zeros(total.shape[1:], F32)

        def add(r):
            if kind == 0:
                weight = begin_of((group - r) * tokens + tokens - 1) == my_first
            else:
                weight = begin_of((group + r) * tokens) == my_last
            state_copy(refs, kind, part, h, r).wait_recv()
            total[h] = total[h] + weight.astype(F32) * refs[part][r, h]

        each_state(kind, False, add)

    def normalise(h):
        loop(1, members, lambda r: o_copy(h, (me + members - r) % members, (me + members - r) % members).wait_recv())
        gather(0, 1, keys, n_row, h)
        feat = (qf[h, 0], qf[h, 1])
        norm = halves(jnp.broadcast_to(n_row[h, 0:1, 0:FEATS], (HEAD_DIM, FEATS)))
        for i in range(tokens // BLOCK):
            t0 = i * BLOCK
            carried = dot_halves(norm, (feat[0][:, t0 : t0 + BLOCK], feat[1][:, t0 : t0 + BLOCK])).T
            inv = 1.0 / (den[h, t0 : t0 + BLOCK, :] + carried)
            den[h, t0 : t0 + BLOCK, :] = inv
            gn_buf[h, t0 : t0 + BLOCK, :] = o_buf[h, t0 : t0 + BLOCK, :] * inv
        g_buf[0, h] = dot_halves(feat, halves(gn_buf[h]))
        each_state(1, True, lambda r: state_copy(grads, 1, 0, h, r).start())
        gather(0, 0, keys, s_sum, h)
        left = halves(s_sum[h].T)
        for i in range(tokens // BLOCK):
            t0 = i * BLOCK
            carried = dot_halves(left, (feat[0][:, t0 : t0 + BLOCK], feat[1][:, t0 : t0 + BLOCK])).T
            attended = (num[h, t0 : t0 + BLOCK, :] + carried) * den[h, t0 : t0 + BLOCK, :]
            gd = -jnp.sum(gn_buf[h, t0 : t0 + BLOCK, :] * attended, axis=1, keepdims=True)
            gd_buf[h, t0 : t0 + BLOCK, :] = jnp.broadcast_to(gd, (BLOCK, LANES))
        norm = dot_halves(halves(gd_buf[h].T[0:8]), feat, 1, 1)
        gd_state[0, h] = jnp.concatenate([norm, jnp.zeros((8, 256 - FEATS), F32)], axis=1)
        each_state(1, True, lambda r: state_copy(grads, 1, 1, h, r).start())

    loop(0, hpd, normalise)

    def column(row):
        return jnp.broadcast_to(row, (LANES, 256)).T[0:FEATS, 0:1]

    far = tokens + LANES
    pos_far = base + lax.broadcasted_iota(jnp.int32, (1, far), 1)
    off_far = jnp.where(pos_far < total_len, pos_far - begin_of(pos_far), 0)

    def back_qk(h):
        return remote(
            dmqk.at[h, :, pl.ds(0, LANES)], dmqk.at[h, :, pl.ds(tokens, LANES)],
            back_send.at[0, h], back_recv.at[0, h], device(prv, me),
        )

    def back_v(h):
        return remote(
            dmv.at[h, pl.ds(0, 8), :], dmv.at[h, pl.ds(tokens, 8), :],
            back_send.at[1, h], back_recv.at[1, h], device(prv, me),
        )

    def out_qk(h, m, slot):
        return remote(sqk.at[m, h], rqk.at[slot, h], out_send.at[0, h, m], out_recv.at[0, h, slot], device(group, m))

    def out_v(h, m, slot):
        return remote(sv.at[m, h], rv.at[slot, h], out_send.at[1, h, m], out_recv.at[1, h, slot], device(group, m))

    def backward(h):
        vh, vl = halves(vm[h])
        v_twice = jnp.concatenate([vh, vh], axis=1)
        qh, ql = halves(q_of(h))
        kh, kl = halves(k_of(h))
        q_both = jnp.concatenate([qh, ql], axis=0)
        k_both = jnp.concatenate([kh, kl], axis=0)
        dvt[h] = jnp.zeros((HEAD_DIM, tokens), F32)
        dmqk[h, 16:32, 0:tokens] = jnp.zeros((16, tokens), F32)
        for i in range(tokens // BLOCK):
            t0, wide = i * BLOCK, (i + 1) * BLOCK
            allowed, u, sc = scores(h, i)
            gn = gn_buf[h, t0 : t0 + BLOCK, :]
            gh, gl = halves(gn)
            ds = dot(jnp.concatenate([gh, gl], axis=1), v_twice[0:wide], 1, 1) + dot(gh, vl[0:wide], 1, 1)
            dx = jnp.where(allowed, (ds + gd_buf[h, t0 : t0 + BLOCK, 0:1]) * u, 0.0)
            dh, dl = halves(dx)
            sh, sl = halves(sc)
            gth, gtl = halves(gn.T)
            dv = dot(jnp.concatenate([gth, gtl], axis=0), sh)
            dvt[h, :, 0:wide] += dv[0:128] + (dv[128:256] + dot(gth, sl))
            dk = dot(q_both[:, t0 : t0 + BLOCK], dh)
            dmqk[h, 16:32, 0:wide] += dk[0:16] + (dk[16:32] + dot(qh[:, t0 : t0 + BLOCK], dl))
            dq = dot(k_both[:, 0:wide], dh, 1, 1)
            dmqk[h, 0:16, t0 : t0 + BLOCK] = dq[0:16] + (dq[16:32] + dot(kh[:, 0:wide], dl, 1, 1))
        gd_row = gd_buf[h].T[0:1]
        dqf = dot_halves(halves(s_sum[h]), halves(gn_buf[h]), 1, 1) + column(n_row[h, 0:1, :]) * gd_row
        dmqk[h, 0:16, 0:tokens] += features_pull(q_of(h), dqf * lead_row)

        gather(1, 0, grads, s_sum, h)
        dv = dvt[h] + dot_halves(halves(s_sum[h].T), (kf[h, 0], kf[h, 1]))
        dmv[h, 0:tokens, :] = dv.T
        back_v(h).start()
        gather(1, 1, grads, n_row, h)
        dkf = dot_halves(halves(s_sum[h]), halves(vm[h]), 1, 1) + column(n_row[h, 0:1, :])
        dmqk[h, 16:32, 0:tokens] += features_pull(k_of(h), dkf * tail_row)
        dmqk[h, :, 0:tokens] = dmqk[h, :, 0:tokens] * (KEY_DIM ** (-0.25))
        back_qk(h).start()

        def drain(r):
            m = (me + r) % members
            qk_copy(h, m, me).wait_send()
            v_copy(h, m, me).wait_send()

        loop(1, members, drain)

        @pl.when(is_last)
        def _():
            def one(m):
                halo_qk(h, m, nxt).wait_send()
                halo_v(h, m, nxt).wait_send()

            loop(0, members, one)

        w_cols, w_rows = taps_of(h)
        sums = [jnp.zeros((1, HEAD_DIM), F32) for _ in range(3)]
        for m in range(members):
            t0 = m * rows
            count = rows + 8
            if m == members - 1:
                back_v(h).wait()
            pcol = base + t0 + lax.broadcasted_iota(jnp.int32, (count, LANES), 0)
            off = jnp.where(pcol < total_len, pcol - begin_of(pcol), 0)
            d0 = dmv[h, t0 : t0 + count, :]
            d1 = jnp.where(off >= 1, d0, 0.0)
            d2 = jnp.where(off >= 2, d0, 0.0)
            sv[m, h] = w_rows[0] * d0[0:rows] + w_rows[1] * d1[1 : rows + 1] + w_rows[2] * d2[2 : rows + 2]
            for j, d in enumerate((d0, d1, d2)):
                past = v_buf[h, t0 + 8 - j : t0 + 8 - j + rows, :]
                sums[j] = sums[j] + jnp.sum(d[0:rows] * past, axis=0, keepdims=True)
        loop(1, members, lambda r: out_v(h, (me + r) % members, me).start())
        back_qk(h).wait()
        dm = dmqk[h]
        dm1 = jnp.where(off_far >= 1, dm, 0.0)
        dm2 = jnp.where(off_far >= 2, dm, 0.0)
        back = (
            w_cols[0] * dm[:, 0:tokens]
            + w_cols[1] * pltpu.roll(dm1, far - 1, 1)[:, 0:tokens]
            + w_cols[2] * pltpu.roll(dm2, far - 2, 1)[:, 0:tokens]
        )
        for m in range(members):
            sqk[m, h] = back[:, m * rows : m * rows + rows]
        loop(1, members, lambda r: out_qk(h, (me + r) % members, me).start())
        lane = lax.broadcasted_iota(jnp.int32, (LANES, LANES), 1)
        square = jnp.zeros((LANES, LANES), F32)
        for j, (d, sig) in enumerate(zip((dm, dm1, dm2), qk_signal(h))):
            tap = jnp.sum(d[:, 0:tokens] * sig, axis=1, keepdims=True)
            tall = jnp.concatenate([tap, jnp.zeros((LANES - 32, 1), F32)], axis=0)
            square = jnp.where(lane == j, tall, square)
        wmsg[group, h, :, LANES:] = square.T[0:8]
        wmsg[group, h, :, 0:LANES] = jnp.concatenate(sums + [jnp.zeros((5, HEAD_DIM), F32)], axis=0)
        rqk[me, h] = sqk[me, h]
        rv[me, h] = sv[me, h]

    loop(0, hpd, backward)

    def w_copy(slot, g):
        return remote(wmsg.at[slot], wmsg.at[slot], w_send.at[g], w_recv.at[slot], device(g, me))

    def t_copy(m, slot):
        return remote(wtot.at[slot], wtot.at[slot], wt_send.at[m], wt_recv.at[slot], device(group, m))

    loop(1, groups, lambda r: w_copy(group, (group + r) % groups).start())
    loop(1, groups, lambda r: w_copy((group + groups - r) % groups, (group + groups - r) % groups).wait_recv())
    wtot[me] = lax.fori_loop(0, groups, lambda g, acc: acc + wmsg[g], jnp.zeros(wmsg.shape[1:], F32))
    loop(1, members, lambda r: t_copy((me + r) % members, me).start())

    for h in range(hpd):
        def take(r):
            m = (me + members - r) % members
            out_v(h, m, m).wait_recv()
            out_qk(h, m, m).wait_recv()

        loop(1, members, take)
        for d in range(members):
            first = WIDTH * (d * hpd + h)
            tall = jnp.concatenate([rqk[d, h], jnp.zeros((96, rows), F32)], axis=0)
            gp_ref[:, first : first + 32] = tall.T[:, 0:32]
            gp_ref[:, first + 32 : first + WIDTH] = rv[d, h]

    def take_taps(r):
        m = (me + members - r) % members
        t_copy(m, m).wait_recv()

    loop(1, members, take_taps)
    for n in range(HEADS):
        d, h = n // hpd, n % hpd
        first = WIDTH * n
        gw_ref[:, first : first + 32] = wtot[d, h, 0:3, LANES : LANES + 32]
        gw_ref[:, first + 32 : first + WIDTH] = wtot[d, h, 0:3, 0:LANES]

    def drain_members(r):
        m = (me + r) % members

        def one(h):
            o_copy(h, m, me).wait_send()
            out_v(h, m, me).wait_send()
            out_qk(h, m, me).wait_send()

        loop(0, hpd, one)
        t_copy(m, me).wait_send()

    loop(1, members, drain_members)
    loop(1, groups, lambda r: w_copy(group, (group + r) % groups).wait_send())

    def drain_states(h):
        for kind, refs in enumerate((keys, grads)):
            for part in range(2):
                each_state(kind, True, lambda r: state_copy(refs, kind, part, h, r).wait_send())

    loop(0, hpd, drain_states)


def on_device(sub, side, groups, projected, out_grads, conv_weight, doc_lengths):
    members = sub * side
    hpd = HEADS // members
    rows = projected.shape[0]
    tokens = rows * members
    reach = max(1, groups // 2)
    vmem = pltpu.VMEM
    dma = pltpu.SemaphoreType.DMA
    scratch = [
        vmem((members, hpd, rows, HEAD_DIM), F32),
        vmem((members, hpd, 32, rows), F32),
        vmem((hpd, tokens + 8, HEAD_DIM), F32),
        vmem((members + 1, hpd, 32, rows), F32),
        vmem((hpd, tokens, HEAD_DIM), F32),
        vmem((members, hpd, 8, HEAD_DIM), F32),
        vmem((members, hpd, 32, LANES), F32),
        vmem((tokens, LANES), jnp.int32),
        vmem((8, tokens), jnp.int32),
        vmem((hpd, tokens, HEAD_DIM), F32),
        vmem((hpd, 32, tokens), F32),
        vmem((hpd, tokens, 64), BF16),
        vmem((hpd, 64, tokens), BF16),
        vmem((hpd, 2, FEATS, tokens), BF16),
        vmem((hpd, 2, FEATS, tokens), BF16),
        vmem((hpd, tokens, LANES), F32),
        vmem((hpd, tokens, LANES), F32),
        vmem((hpd, tokens, LANES), F32),
        vmem((hpd, tokens, LANES), F32),
        vmem((reach + 1, hpd, FEATS, HEAD_DIM), F32),
        vmem((reach + 1, hpd, 8, 256), F32),
        vmem((reach + 1, hpd, FEATS, HEAD_DIM), F32),
        vmem((reach + 1, hpd, 8, 256), F32),
        vmem((hpd, 8, 256), F32),
        vmem((hpd, FEATS, HEAD_DIM), F32),
        vmem((hpd, tokens + 8, HEAD_DIM), F32),
        vmem((hpd, 32, tokens + LANES), F32),
        vmem((hpd, HEAD_DIM, tokens), F32),
        vmem((members, hpd, rows, HEAD_DIM), F32),
        vmem((members, hpd, 32, rows), F32),
        vmem((groups, hpd, 8, 2 * LANES), F32),
        vmem((members, hpd, 8, 2 * LANES), F32),
        dma((3, hpd, members)),
        dma((3, hpd, members)),
        dma((2, hpd, members)),
        dma((2, hpd)),
        dma((2, 2, hpd, reach + 1)),
        dma((2, 2, hpd, reach + 1)),
        dma((2, hpd)),
        dma((2, hpd)),
        dma((2, hpd, members)),
        dma((2, hpd, members)),
        dma((groups,)),
        dma((groups,)),
        dma((members,)),
        dma((members,)),
    ]
    spec = pl.BlockSpec(memory_space=pltpu.VMEM)
    return pl.pallas_call(
        functools.partial(kernel, sub, side, groups, reach, "seq", "head"),
        out_shape=(
            jax.ShapeDtypeStruct(projected.shape, F32),
            jax.ShapeDtypeStruct(conv_weight.shape, F32),
        ),
        in_specs=[pl.BlockSpec(memory_space=pltpu.SMEM), spec, spec, spec],
        out_specs=(spec, spec),
        scratch_shapes=scratch,
        compiler_params=pltpu.CompilerParams(
            collective_id=0, has_side_effects=True, vmem_limit_bytes=60 * 1024 * 1024
        ),
        name="layer_backward",
    )(doc_lengths, projected, out_grads, conv_weight)


def solution(mesh):
    side = mesh.shape["head"]
    sub = max(1, MEMBERS // side)
    groups = mesh.shape["seq"] // sub
    return jax.shard_map(
        functools.partial(on_device, sub, side, groups),
        mesh=mesh,
        in_specs=(P(("seq", "head"), None), P(("seq", "head"), None), P(), P()),
        out_specs=(P(("seq", "head"), None), P()),
        check_vma=False,
    )
```

time: 96.5 us -> 71.1 us (0.74)
  the two profiles are of different devices: /device:TPU:21 before, /device:TPU:0 now
where the time goes in v2:
time: 71.1 us; the launch traced here: 70.9 us
  Pallas kernels  67.2 us (95%)
  local copies, waits for them, and re-layouts  3.1 us (4%)
    pallas_call x1, Pallas kernels, on_device(): pl.pallas_call(functools.partial(kernel, sub, side, groups, reach, 'seq',...  67.2 us
    unnamed x4, local copies, waits for them, and re-layouts  3.1 us

profile of v2, /device:TPU:0, one launch (start us, length us, event | category | flops | bytes accessed | tf_op | source)
XLA Modules:
  0.0 70.9 jit_solution(6499145667885468473)
XLA Ops:
  0.6 67.2 %layer_backward.1 = (f32[128,2560]{1,0:T(8,128)}, f32[3,2560]{1,0:T(4,128)}) custom-call(s32[4]{0:T(128)} %docs_ref.1, f32[128,2560]{1,0:T(8,128)} %p_ref.1, f32[128,2048]{1,0:T(8,128)} %o_ref.1, f32[3,2560]{1,0:T(4,128)} %w_ref.1), custom_call_target="tpu_custom_call" | custom-call | tf_op jit(solution)/shard_map/layer_backward/pallas_call | solution.py:589
  67.8 0.0 copy-start
  67.8 2.5 %copy.8 = f32[128,2560]{1,0:T(8,128)} copy(f32[128,2560]{1,0:T(8,128)} %get-tuple-element.4) | data formatting | bytes 2621440
  70.3 0.0 copy-done
  70.3 0.6 copy.9
Async XLA Ops:
  67.8 2.5 %copy-start = (f32[3,2560]{1,0:T(4,128)S(1)}, f32[3,2560]{1,0:T(4,128)}, u32[]{:S(2)}) copy-start(f32[3,2560]{1,0:T(4,128)} %get-tuple-element.5) | copy-start | bytes 92164

commit v3 on v2

--- a/solution.py
+++ b/solution.py
@@ -61,14 +61,14 @@
 def kernel(
     sub, side, groups, reach, seq_name, head_name,
     docs_ref, p_ref, o_ref, w_ref,
-    gp_ref, gw_ref,
+    rv, rqk, wt_ref,
     sv, sqk, v_buf, qk_buf, o_buf, wv_all, wqk_all,
     bcol, brow, vm, qkm, qrow, kst, qf, kf,
     num, den, gn_buf, gd_buf,
     s_buf, n_buf, g_buf, gd_state, n_row, s_sum,
-    dmv, dmqk, dvt, rv, rqk, wmsg, wtot,
+    u_buf, sc_buf, dmv, dmqk, dvt, wmsg, wtot,
     in_send, in_recv, halo_send, halo_recv, state_send, state_recv,
-    back_send, back_recv, out_send, out_recv, w_send, w_recv, wt_send, wt_recv,
+    back_send, back_recv, out_send, out_recv, w_send, w_recv, wt_send, wt_recv, own_sem,
 ):
     members = sub * side
     hpd = HEADS // members
@@ -114,15 +114,16 @@
     def _():
         greet(device(prv, members - 1))
 
-    for n in range(HEADS):
-        d, h = n // hpd, n % hpd
-        first = WIDTH * n
-        tile = (first // LANES) * LANES
-        off = first - tile
-        turned = p_ref[:, tile : tile + LANES].T
-        sqk[d, h] = turned[off : off + 32, :]
-        sv[d, h] = p_ref[:, first + 32 : first + WIDTH]
-
+    def pack(h):
+        for d in range(members):
+            first = WIDTH * (d * hpd + h)
+            tile = (first // LANES) * LANES
+            off = first - tile
+            turned = p_ref[:, tile : tile + LANES].T
+            sqk[d, h] = turned[off : off + 32, :]
+            sv[d, h] = p_ref[:, first + 32 : first + WIDTH]
+
+    pack(0)
     pl.semaphore_wait(barrier, members - 1 + groups - 1 + jnp.where(is_last, members - 1, 1))
 
     def qk_copy(h, m, slot):
@@ -171,7 +172,10 @@
 
         loop(1, members, one)
 
-    loop(0, hpd, send_in)
+    send_in(0)
+    for h in range(1, hpd):
+        pack(h)
+        send_in(h)
     loop(0, hpd, lambda h: loop(1, members, lambda r: o_copy(h, (me + r) % members, me).start()))
 
     def keep_own(h):
@@ -281,8 +285,6 @@
         s_buf[0, h] = dot_halves(feat, halves(vm[h]))
         each_state(0, True, lambda r: state_copy(keys, 0, 0, h, r).start())
 
-    loop(0, hpd, arrive)
-
     def scores(h, i):
         wide = (i + 1) * BLOCK
         t0 = i * BLOCK
@@ -291,7 +293,7 @@
         t_pos = t0 + lax.broadcasted_iota(jnp.int32, (BLOCK, wide), 0)
         begin = bcol[t0 : t0 + BLOCK, 0:1] - base
         allowed = (s_pos >= begin) & (s_pos <= t_pos)
-        return allowed, u, jnp.where(allowed, 0.5 + 0.5 * (u * u), 0.0)
+        return jnp.where(allowed, u, 0.0), jnp.where(allowed, 0.5 + 0.5 * (u * u), 0.0)
 
     def forward(h):
         q = q_of(h)
@@ -303,13 +305,20 @@
         both = jnp.concatenate([vh, vl], axis=1)
         for i in range(tokens // BLOCK):
             t0, wide = i * BLOCK, (i + 1) * BLOCK
-            _, _, sc = scores(h, i)
+            u, sc = scores(h, i)
             sh, sl = halves(sc)
+            u_buf[h, t0 : t0 + BLOCK, 0:wide] = u
+            sc_buf[h, 0, t0 : t0 + BLOCK, 0:wide] = sh
+            sc_buf[h, 1, t0 : t0 + BLOCK, 0:wide] = sl
             wide_num = dot(sh, both[0:wide])
             num[h, t0 : t0 + BLOCK, :] = wide_num[:, 0:128] + (wide_num[:, 128:256] + dot(sl, vh[0:wide]))
             den[h, t0 : t0 + BLOCK, :] = jnp.broadcast_to(jnp.sum(sc, axis=1, keepdims=True), (BLOCK, LANES))
 
-    loop(0, hpd, forward)
+    def first_pass(h):
+        arrive(h)
+        forward(h)
+
+    loop(0, hpd, first_pass)
 
     def gather(kind, part, refs, total, h):
         total[h] = jnp.zeros(total.shape[1:], F32)
@@ -376,6 +385,12 @@
     def out_v(h, m, slot):
         return remote(sv.at[m, h], rv.at[slot, h], out_send.at[1, h, m], out_recv.at[1, h, slot], device(group, m))
 
+    def own_copies(h):
+        return (
+            pltpu.make_async_copy(sv.at[me, h], rv.at[me, h], own_sem.at[0, h]),
+            pltpu.make_async_copy(sqk.at[me, h], rqk.at[me, h], own_sem.at[1, h]),
+        )
+
     def backward(h):
         vh, vl = halves(vm[h])
         v_twice = jnp.concatenate([vh, vh], axis=1)
@@ -387,13 +402,11 @@
         dmqk[h, 16:32, 0:tokens] = jnp.zeros((16, tokens), F32)
         for i in range(tokens // BLOCK):
             t0, wide = i * BLOCK, (i + 1) * BLOCK
-            allowed, u, sc = scores(h, i)
             gn = gn_buf[h, t0 : t0 + BLOCK, :]
             gh, gl = halves(gn)
             ds = dot(jnp.concatenate([gh, gl], axis=1), v_twice[0:wide], 1, 1) + dot(gh, vl[0:wide], 1, 1)
-            dx = jnp.where(allowed, (ds + gd_buf[h, t0 : t0 + BLOCK, 0:1]) * u, 0.0)
-            dh, dl = halves(dx)
-            sh, sl = halves(sc)
+            dh, dl = halves((ds + gd_buf[h, t0 : t0 + BLOCK, 0:1]) * u_buf[h, t0 : t0 + BLOCK, 0:wide])
+            sh, sl = sc_buf[h, 0, t0 : t0 + BLOCK, 0:wide], sc_buf[h, 1, t0 : t0 + BLOCK, 0:wide]
             gth, gtl = halves(gn.T)
             dv = dot(jnp.concatenate([gth, gtl], axis=0), sh)
             dvt[h, :, 0:wide] += dv[0:128] + (dv[128:256] + dot(gth, sl))
@@ -467,8 +480,8 @@
             square = jnp.where(lane == j, tall, square)
         wmsg[group, h, :, LANES:] = square.T[0:8]
         wmsg[group, h, :, 0:LANES] = jnp.concatenate(sums + [jnp.zeros((5, HEAD_DIM), F32)], axis=0)
-        rqk[me, h] = sqk[me, h]
-        rv[me, h] = sv[me, h]
+        for c in own_copies(h):
+            c.start()
 
     loop(0, hpd, backward)
 
@@ -483,29 +496,24 @@
     wtot[me] = lax.fori_loop(0, groups, lambda g, acc: acc + wmsg[g], jnp.zeros(wmsg.shape[1:], F32))
     loop(1, members, lambda r: t_copy((me + r) % members, me).start())
 
-    for h in range(hpd):
-        def take(r):
+    def take(h):
+        def one(r):
             m = (me + members - r) % members
             out_v(h, m, m).wait_recv()
             out_qk(h, m, m).wait_recv()
 
-        loop(1, members, take)
-        for d in range(members):
-            first = WIDTH * (d * hpd + h)
-            tall = jnp.concatenate([rqk[d, h], jnp.zeros((96, rows), F32)], axis=0)
-            gp_ref[:, first : first + 32] = tall.T[:, 0:32]
-            gp_ref[:, first + 32 : first + WIDTH] = rv[d, h]
+        loop(1, members, one)
+        for c in own_copies(h):
+            c.wait()
+
+    loop(0, hpd, take)
 
     def take_taps(r):
         m = (me + members - r) % members
         t_copy(m, m).wait_recv()
 
     loop(1, members, take_taps)
-    for n in range(HEADS):
-        d, h = n // hpd, n % hpd
-        first = WIDTH * n
-        gw_ref[:, first : first + 32] = wtot[d, h, 0:3, LANES : LANES + 32]
-        gw_ref[:, first + 32 : first + WIDTH] = wtot[d, h, 0:3, 0:LANES]
+    wt_ref[...] = wtot[...]
 
     def drain_members(r):
         m = (me + r) % members
@@ -527,6 +535,18 @@
                 each_state(kind, True, lambda r: state_copy(refs, kind, part, h, r).wait_send())
 
     loop(0, hpd, drain_states)
+
+
+def unpack(hpd, v_ref, qk_ref, taps_ref, gp_ref, gw_ref):
+    rows = gp_ref.shape[0]
+    for n in range(2 * hpd):
+        d, h = n // hpd, n % hpd
+        first = WIDTH * n
+        tall = jnp.concatenate([qk_ref[d, h], jnp.zeros((LANES - 32, rows), F32)], axis=0)
+        gp_ref[:, first : first + 32] = tall.T[:, 0:32]
+        gp_ref[:, first + 32 : first + WIDTH] = v_ref[d, h]
+        gw_ref[:, first : first + 32] = taps_ref[d, h, 0:3, LANES : LANES + 32]
+        gw_ref[:, first + 32 : first + WIDTH] = taps_ref[d, h, 0:3, 0:LANES]
 
 
 def on_device(sub, side, groups, projected, out_grads, conv_weight, doc_lengths):
@@ -563,11 +583,11 @@
         vmem((reach + 1, hpd, 8, 256), F32),
         vmem((hpd, 8, 256), F32),
         vmem((hpd, FEATS, HEAD_DIM), F32),
+        vmem((hpd, tokens, tokens), F32),
+        vmem((hpd, 2, tokens, tokens), BF16),
         vmem((hpd, tokens + 8, HEAD_DIM), F32),
         vmem((hpd, 32, tokens + LANES), F32),
         vmem((hpd, HEAD_DIM, tokens), F32),
-        vmem((members, hpd, rows, HEAD_DIM), F32),
-        vmem((members, hpd, 32, rows), F32),
         vmem((groups, hpd, 8, 2 * LANES), F32),
         vmem((members, hpd, 8, 2 * LANES), F32),
         dma((3, hpd, members)),
@@ -584,22 +604,37 @@
         dma((groups,)),
         dma((members,)),
         dma((members,)),
+        dma((2, hpd)),
     ]
     spec = pl.BlockSpec(memory_space=pltpu.VMEM)
-    return pl.pallas_call(
+    returned = (members, hpd, rows, HEAD_DIM), (members, hpd, 32, rows), (members, hpd, 8, 2 * LANES)
+    anywhere = pl.BlockSpec(memory_space=pl.ANY)
+    values, columns, taps = pl.pallas_call(
         functools.partial(kernel, sub, side, groups, reach, "seq", "head"),
-        out_shape=(
-            jax.ShapeDtypeStruct(projected.shape, F32),
-            jax.ShapeDtypeStruct(conv_weight.shape, F32),
-        ),
+        out_shape=tuple(jax.ShapeDtypeStruct(shape, F32) for shape in returned),
         in_specs=[pl.BlockSpec(memory_space=pltpu.SMEM), spec, spec, spec],
-        out_specs=(spec, spec),
+        out_specs=(anywhere, anywhere, spec),
         scratch_shapes=scratch,
         compiler_params=pltpu.CompilerParams(
             collective_id=0, has_side_effects=True, vmem_limit_bytes=60 * 1024 * 1024
         ),
         name="layer_backward",
     )(doc_lengths, projected, out_grads, conv_weight)
+    pair = 2 * hpd * WIDTH
+    return pl.pallas_call(
+        functools.partial(unpack, hpd),
+        grid=(members // 2,),
+        out_shape=(
+            jax.ShapeDtypeStruct(projected.shape, F32),
+            jax.ShapeDtypeStruct(conv_weight.shape, F32),
+        ),
+        in_specs=[
+            pl.BlockSpec((2,) + shape[1:], lambda i: (i, 0, 0, 0)) for shape in returned
+        ],
+        out_specs=(pl.BlockSpec((rows, pair), lambda i: (0, i)), pl.BlockSpec((3, pair), lambda i: (0, i))),
+        compiler_params=pltpu.CompilerParams(vmem_limit_bytes=60 * 1024 * 1024),
+        name="unpack_heads",
+    )(values, columns, taps)
 
 
 def solution(mesh):

time: 71.1 us -> 70.4 us (level)
  local copies, waits for them, and re-layouts: 3.1 us -> 0 us
  Pallas kernels: 67.2 us -> 69.5 us
    pallas_call x0 -> x1, Pallas kernels: none -> 4.01 us  [on_device(): pl.pallas_call(functools.partial(unpack, hpd), grid=(members // 2,), out_...]
    unnamed x4 -> x0, local copies, waits for them, and re-layouts: 3.1 us -> none
    pallas_call x1, Pallas kernels: 67.2 us -> 65.5 us  [on_device(): pl.pallas_call(functools.partial(kernel, sub, side, groups, reach, 'seq',...]
where the time goes in v3:
time: 70.4 us; the launch traced here: 70.1 us
  Pallas kernels  69.5 us (99%)
    pallas_call x1, Pallas kernels, on_device(): pl.pallas_call(functools.partial(kernel, sub, side, groups, reach, 'seq',...  65.5 us
    pallas_call x1, Pallas kernels, on_device(): pl.pallas_call(functools.partial(unpack, hpd), grid=(members // 2,), out_...  4.01 us

profile of v3, /device:TPU:0, one launch (start us, length us, event | category | flops | bytes accessed | tf_op | source)
XLA Modules:
  0.0 70.1 jit_solution(8178926177572478462)
XLA Ops:
  0.6 65.5 %layer_backward.1 = (f32[8,2,128,128]{3,2,1,0:T(8,128)}, f32[8,2,32,128]{3,2,1,0:T(8,128)}, f32[8,2,8,256]{3,2,1,0:T(8,128)}) custom-call(s32[4]{0:T(128)} %docs_ref.1, f32[128,2560]{1,0:T(8,128)} %p_ref.1, f32[128,2048]{1,0:T(8,128)} %o_ref.1, f32[3,2560]{1,0:T(4,128)} %w_ref.1), custom_call_target="tpu_custom_call" | custom-call | tf_op jit(solution)/shard_map/layer_backward/pallas_call | solution.py:612
  66.1 4.0 %unpack_heads.1 = (f32[128,2560]{1,0:T(8,128)}, f32[3,2560]{1,0:T(4,128)}) custom-call(f32[8,2,128,128]{3,2,1,0:T(8,128)} %get-tuple-element.5.v_ref, f32[8,2,32,128]{3,2,1,0:T(8,128)} %get-tuple-element.6.qk_ref, f32[8,2,8,256]{3,2,1,0:T(8,128)} %get-tuple-element.7.taps_ref), custom_call_target="tpu_custom_call" | custom-call | tf_op jit(solution)/shard_map/unpack_heads/pallas_call | solution.py:624

commit v4 on v3

--- a/solution.py
+++ b/solution.py
@@ -171,12 +171,12 @@
             v_copy(h, m, me).start()
 
         loop(1, members, one)
+        loop(1, members, lambda r: o_copy(h, (me + r) % members, me).start())
 
     send_in(0)
     for h in range(1, hpd):
         pack(h)
         send_in(h)
-    loop(0, hpd, lambda h: loop(1, members, lambda r: o_copy(h, (me + r) % members, me).start()))
 
     def keep_own(h):
         qk_buf[me + 1, h] = sqk[me, h]
@@ -314,12 +314,6 @@
             num[h, t0 : t0 + BLOCK, :] = wide_num[:, 0:128] + (wide_num[:, 128:256] + dot(sl, vh[0:wide]))
             den[h, t0 : t0 + BLOCK, :] = jnp.broadcast_to(jnp.sum(sc, axis=1, keepdims=True), (BLOCK, LANES))
 
-    def first_pass(h):
-        arrive(h)
-        forward(h)
-
-    loop(0, hpd, first_pass)
-
     def gather(kind, part, refs, total, h):
         total[h] = jnp.zeros(total.shape[1:], F32)
 
@@ -357,8 +351,6 @@
         norm = dot_halves(halves(gd_buf[h].T[0:8]), feat, 1, 1)
         gd_state[0, h] = jnp.concatenate([norm, jnp.zeros((8, 256 - FEATS), F32)], axis=1)
         each_state(1, True, lambda r: state_copy(grads, 1, 1, h, r).start())
-
-    loop(0, hpd, normalise)
 
     def column(row):
         return jnp.broadcast_to(row, (LANES, 256)).T[0:FEATS, 0:1]
@@ -418,6 +410,7 @@
         dqf = dot_halves(halves(s_sum[h]), halves(gn_buf[h]), 1, 1) + column(n_row[h, 0:1, :]) * gd_row
         dmqk[h, 0:16, 0:tokens] += features_pull(q_of(h), dqf * lead_row)
 
+    def finish(h):
         gather(1, 0, grads, s_sum, h)
         dv = dvt[h] + dot_halves(halves(s_sum[h].T), (kf[h, 0], kf[h, 1]))
         dmv[h, 0:tokens, :] = dv.T
@@ -483,7 +476,22 @@
         for c in own_copies(h):
             c.start()
 
-    loop(0, hpd, backward)
+    def stage(i):
+        @pl.when(i < hpd)
+        def _():
+            arrive(i)
+            forward(i)
+
+        @pl.when(i > 0)
+        def _():
+            finish(i - 1)
+
+        @pl.when(i < hpd)
+        def _():
+            normalise(i)
+            backward(i)
+
+    loop(0, hpd + 1, stage)
 
     def w_copy(slot, g):
         return remote(wmsg.at[slot], wmsg.at[slot], w_send.at[g], w_recv.at[slot], device(g, me))
@@ -537,16 +545,42 @@
     loop(0, hpd, drain_states)
 
 
-def unpack(hpd, v_ref, qk_ref, taps_ref, gp_ref, gw_ref):
+def unpack(hpd, v_any, qk_any, taps_ref, gp_any, gw_ref, v_ref, qk_ref, gp_ref, v_sem, qk_sem, out_sem):
     rows = gp_ref.shape[0]
-    for n in range(2 * hpd):
+    pairs = v_ref.shape[0] // 2
+    wide = 2 * hpd * WIDTH
+
+    def loads(i):
+        at = pl.ds(2 * i, 2)
+        return (
+            pltpu.make_async_copy(v_any.at[at], v_ref.at[at], v_sem.at[i]),
+            pltpu.make_async_copy(qk_any.at[at], qk_ref.at[at], qk_sem.at[i]),
+        )
+
+    def store(i):
+        at = pl.ds(i * wide, wide)
+        return pltpu.make_async_copy(gp_ref.at[:, at], gp_any.at[:, at], out_sem.at[i])
+
+    for i in range(pairs):
+        for c in loads(i):
+            c.start()
+    for n in range(HEADS):
         d, h = n // hpd, n % hpd
         first = WIDTH * n
-        tall = jnp.concatenate([qk_ref[d, h], jnp.zeros((LANES - 32, rows), F32)], axis=0)
-        gp_ref[:, first : first + 32] = tall.T[:, 0:32]
-        gp_ref[:, first + 32 : first + WIDTH] = v_ref[d, h]
         gw_ref[:, first : first + 32] = taps_ref[d, h, 0:3, LANES : LANES + 32]
         gw_ref[:, first + 32 : first + WIDTH] = taps_ref[d, h, 0:3, 0:LANES]
+    for i in range(pairs):
+        for c in loads(i):
+            c.wait()
+        for n in range(2 * hpd * i, 2 * hpd * (i + 1)):
+            d, h = n // hpd, n % hpd
+            first = WIDTH * n
+            tall = jnp.concatenate([qk_ref[d, h], jnp.zeros((LANES - 32, rows), F32)], axis=0)
+            gp_ref[:, first : first + 32] = tall.T[:, 0:32]
+            gp_ref[:, first + 32 : first + WIDTH] = v_ref[d, h]
+        store(i).start()
+    for i in range(pairs):
+        store(i).wait()
 
 
 def on_device(sub, side, groups, projected, out_grads, conv_weight, doc_lengths):
@@ -620,18 +654,23 @@
         ),
         name="layer_backward",
     )(doc_lengths, projected, out_grads, conv_weight)
-    pair = 2 * hpd * WIDTH
+    pairs = members // 2
     return pl.pallas_call(
         functools.partial(unpack, hpd),
-        grid=(members // 2,),
         out_shape=(
             jax.ShapeDtypeStruct(projected.shape, F32),
             jax.ShapeDtypeStruct(conv_weight.shape, F32),
         ),
-        in_specs=[
-            pl.BlockSpec((2,) + shape[1:], lambda i: (i, 0, 0, 0)) for shape in returned
+        in_specs=[anywhere, anywhere, spec],
+        out_specs=(anywhere, spec),
+        scratch_shapes=[
+            vmem(returned[0], F32),
+            vmem(returned[1], F32),
+            vmem(projected.shape, F32),
+            dma((pairs,)),
+            dma((pairs,)),
+            dma((pairs,)),
         ],
-        out_specs=(pl.BlockSpec((rows, pair), lambda i: (0, i)), pl.BlockSpec((3, pair), lambda i: (0, i))),
         compiler_params=pltpu.CompilerParams(vmem_limit_bytes=60 * 1024 * 1024),
         name="unpack_heads",
     )(values, columns, taps)

time: 70.4 us -> 67.3 us (0.956)
  Pallas kernels: 69.5 us -> 66.4 us
    pallas_call x1, Pallas kernels: 65.5 us -> 62.1 us  [on_device(): pl.pallas_call(functools.partial(kernel, sub, side, groups, reach, 'seq',...]
where the time goes in v4:
time: 67.3 us; the launch traced here: 67.1 us
  Pallas kernels  66.4 us (99%)
    pallas_call x1, Pallas kernels, on_device(): pl.pallas_call(functools.partial(kernel, sub, side, groups, reach, 'seq',...  62.1 us
    pallas_call x1, Pallas kernels, on_device(): pl.pallas_call(functools.partial(unpack, hpd), out_shape=(jax.ShapeDtypeS...  4.37 us

profile of v4, /device:TPU:0, one launch (start us, length us, event | category | flops | bytes accessed | tf_op | source)
XLA Modules:
  0.0 67.1 jit_solution(1988894655195758028)
XLA Ops:
  0.6 62.1 %layer_backward.1 = (f32[8,2,128,128]{3,2,1,0:T(8,128)}, f32[8,2,32,128]{3,2,1,0:T(8,128)}, f32[8,2,8,256]{3,2,1,0:T(8,128)}) custom-call(s32[4]{0:T(128)} %docs_ref.1, f32[128,2560]{1,0:T(8,128)} %p_ref.1, f32[128,2048]{1,0:T(8,128)} %o_ref.1, f32[3,2560]{1,0:T(4,128)} %w_ref.1), custom_call_target="tpu_custom_call" | custom-call | tf_op jit(solution)/shard_map/layer_backward/pallas_call | solution.py:646
  62.7 4.4 %unpack_heads.1 = (f32[128,2560]{1,0:T(8,128)}, f32[3,2560]{1,0:T(4,128)}) custom-call(f32[8,2,128,128]{3,2,1,0:T(8,128)} %get-tuple-element.5.v_any, f32[8,2,32,128]{3,2,1,0:T(8,128)} %get-tuple-element.6.qk_any, f32[8,2,8,256]{3,2,1,0:T(8,128)} %get-tuple-element.7.taps_ref), custom_call_target="tpu_custom_call" | custom-call | tf_op jit(solution)/shard_map/unpack_heads/pallas_call | solution.py:658

commit v5 on v4

--- a/solution.py
+++ b/solution.py
@@ -64,7 +64,7 @@
     rv, rqk, wt_ref,
     sv, sqk, v_buf, qk_buf, o_buf, wv_all, wqk_all,
     bcol, brow, vm, qkm, qrow, kst, qf, kf,
-    num, den, gn_buf, gd_buf,
+    num, den, gn_buf, gd_buf, gd_row,
     s_buf, n_buf, g_buf, gd_state, n_row, s_sum,
     u_buf, sc_buf, dmv, dmqk, dvt, wmsg, wtot,
     in_send, in_recv, halo_send, halo_recv, state_send, state_recv,
@@ -117,12 +117,13 @@
     def pack(h):
         for d in range(members):
             first = WIDTH * (d * hpd + h)
-            tile = (first // LANES) * LANES
-            off = first - tile
-            turned = p_ref[:, tile : tile + LANES].T
-            sqk[d, h] = turned[off : off + 32, :]
             sv[d, h] = p_ref[:, first + 32 : first + WIDTH]
 
+    for n in range(0, HEADS, 4):
+        four = [p_ref[:, WIDTH * k : WIDTH * k + 32] for k in range(n, n + 4)]
+        turned = jnp.concatenate(four, axis=1).T
+        for k in range(4):
+            sqk[(n + k) // hpd, (n + k) % hpd] = turned[32 * k : 32 * k + 32, :]
     pack(0)
     pl.semaphore_wait(barrier, members - 1 + groups - 1 + jnp.where(is_last, members - 1, 1))
 
@@ -331,10 +332,10 @@
         loop(1, members, lambda r: o_copy(h, (me + members - r) % members, (me + members - r) % members).wait_recv())
         gather(0, 1, keys, n_row, h)
         feat = (qf[h, 0], qf[h, 1])
-        norm = halves(jnp.broadcast_to(n_row[h, 0:1, 0:FEATS], (HEAD_DIM, FEATS)))
+        norm = halves(n_row[h, :, 0:FEATS])
         for i in range(tokens // BLOCK):
             t0 = i * BLOCK
-            carried = dot_halves(norm, (feat[0][:, t0 : t0 + BLOCK], feat[1][:, t0 : t0 + BLOCK])).T
+            carried = dot_halves(norm, (feat[0][:, t0 : t0 + BLOCK], feat[1][:, t0 : t0 + BLOCK])).T[:, 0:1]
             inv = 1.0 / (den[h, t0 : t0 + BLOCK, :] + carried)
             den[h, t0 : t0 + BLOCK, :] = inv
             gn_buf[h, t0 : t0 + BLOCK, :] = o_buf[h, t0 : t0 + BLOCK, :] * inv
@@ -346,14 +347,18 @@
             t0 = i * BLOCK
             carried = dot_halves(left, (feat[0][:, t0 : t0 + BLOCK], feat[1][:, t0 : t0 + BLOCK])).T
             attended = (num[h, t0 : t0 + BLOCK, :] + carried) * den[h, t0 : t0 + BLOCK, :]
-            gd = -jnp.sum(gn_buf[h, t0 : t0 + BLOCK, :] * attended, axis=1, keepdims=True)
+            product = gn_buf[h, t0 : t0 + BLOCK, :] * attended
+            gd = -jnp.sum(product, axis=1, keepdims=True)
             gd_buf[h, t0 : t0 + BLOCK, :] = jnp.broadcast_to(gd, (BLOCK, LANES))
-        norm = dot_halves(halves(gd_buf[h].T[0:8]), feat, 1, 1)
+            ones = jnp.ones((8, HEAD_DIM), BF16)
+            high, low = halves(product)
+            gd_row[h, :, t0 : t0 + BLOCK] = -(dot(ones, high, 1, 1) + dot(ones, low, 1, 1))
+        norm = dot_halves(halves(gd_row[h]), feat, 1, 1)
         gd_state[0, h] = jnp.concatenate([norm, jnp.zeros((8, 256 - FEATS), F32)], axis=1)
         each_state(1, True, lambda r: state_copy(grads, 1, 1, h, r).start())
 
     def column(row):
-        return jnp.broadcast_to(row, (LANES, 256)).T[0:FEATS, 0:1]
+        return row.T[0:FEATS, 0:1]
 
     far = tokens + LANES
     pos_far = base + lax.broadcasted_iota(jnp.int32, (1, far), 1)
@@ -406,8 +411,7 @@
             dmqk[h, 16:32, 0:wide] += dk[0:16] + (dk[16:32] + dot(qh[:, t0 : t0 + BLOCK], dl))
             dq = dot(k_both[:, 0:wide], dh, 1, 1)
             dmqk[h, 0:16, t0 : t0 + BLOCK] = dq[0:16] + (dq[16:32] + dot(kh[:, 0:wide], dl, 1, 1))
-        gd_row = gd_buf[h].T[0:1]
-        dqf = dot_halves(halves(s_sum[h]), halves(gn_buf[h]), 1, 1) + column(n_row[h, 0:1, :]) * gd_row
+        dqf = dot_halves(halves(s_sum[h]), halves(gn_buf[h]), 1, 1) + column(n_row[h]) * gd_row[h, 0:1, :]
         dmqk[h, 0:16, 0:tokens] += features_pull(q_of(h), dqf * lead_row)
 
     def finish(h):
@@ -416,7 +420,7 @@
         dmv[h, 0:tokens, :] = dv.T
         back_v(h).start()
         gather(1, 1, grads, n_row, h)
-        dkf = dot_halves(halves(s_sum[h]), halves(vm[h]), 1, 1) + column(n_row[h, 0:1, :])
+        dkf = dot_halves(halves(s_sum[h]), halves(vm[h]), 1, 1) + column(n_row[h])
         dmqk[h, 16:32, 0:tokens] += features_pull(k_of(h), dkf * tail_row)
         dmqk[h, :, 0:tokens] = dmqk[h, :, 0:tokens] * (KEY_DIM ** (-0.25))
         back_qk(h).start()
@@ -546,7 +550,6 @@
 
 
 def unpack(hpd, v_any, qk_any, taps_ref, gp_any, gw_ref, v_ref, qk_ref, gp_ref, v_sem, qk_sem, out_sem):
-    rows = gp_ref.shape[0]
     pairs = v_ref.shape[0] // 2
     wide = 2 * hpd * WIDTH
 
@@ -572,12 +575,13 @@
     for i in range(pairs):
         for c in loads(i):
             c.wait()
-        for n in range(2 * hpd * i, 2 * hpd * (i + 1)):
-            d, h = n // hpd, n % hpd
-            first = WIDTH * n
-            tall = jnp.concatenate([qk_ref[d, h], jnp.zeros((LANES - 32, rows), F32)], axis=0)
-            gp_ref[:, first : first + 32] = tall.T[:, 0:32]
-            gp_ref[:, first + 32 : first + WIDTH] = v_ref[d, h]
+        for n in range(2 * hpd * i, 2 * hpd * (i + 1), 4):
+            heads = [((n + k) // hpd, (n + k) % hpd) for k in range(4)]
+            turned = jnp.concatenate([qk_ref[d, h] for d, h in heads], axis=0).T
+            pieces = []
+            for k, (d, h) in enumerate(heads):
+                pieces += [turned[:, 32 * k : 32 * k + 32], v_ref[d, h]]
+            gp_ref[:, WIDTH * n : WIDTH * (n + 4)] = jnp.concatenate(pieces, axis=1)
         store(i).start()
     for i in range(pairs):
         store(i).wait()
@@ -611,6 +615,7 @@
         vmem((hpd, tokens, LANES), F32),
         vmem((hpd, tokens, LANES), F32),
         vmem((hpd, tokens, LANES), F32),
+        vmem((hpd, 8, tokens), F32),
         vmem((reach + 1, hpd, FEATS, HEAD_DIM), F32),
         vmem((reach + 1, hpd, 8, 256), F32),
         vmem((reach + 1, hpd, FEATS, HEAD_DIM), F32),

time: 67.3 us -> 67.8 us (level)
    pallas_call x1, Pallas kernels: 62.1 us -> 63.1 us  [on_device(): pl.pallas_call(functools.partial(kernel, sub, side, groups, reach, 'seq',...]
where the time goes in v5:
time: 67.8 us; the launch traced here: 67.6 us
  Pallas kernels  67 us (99%)
    pallas_call x1, Pallas kernels, on_device(): pl.pallas_call(functools.partial(kernel, sub, side, groups, reach, 'seq',...  63.1 us
    pallas_call x1, Pallas kernels, on_device(): pl.pallas_call(functools.partial(unpack, hpd), out_shape=(jax.ShapeDtypeS...  3.9 us

profile of v5, /device:TPU:0, one launch (start us, length us, event | category | flops | bytes accessed | tf_op | source)
XLA Modules:
  0.0 67.6 jit_solution(18151746897227938372)
XLA Ops:
  0.6 63.1 %layer_backward.1 = (f32[8,2,128,128]{3,2,1,0:T(8,128)}, f32[8,2,32,128]{3,2,1,0:T(8,128)}, f32[8,2,8,256]{3,2,1,0:T(8,128)}) custom-call(s32[4]{0:T(128)} %docs_ref.1, f32[128,2560]{1,0:T(8,128)} %p_ref.1, f32[128,2048]{1,0:T(8,128)} %o_ref.1, f32[3,2560]{1,0:T(4,128)} %w_ref.1), custom_call_target="tpu_custom_call" | custom-call | tf_op jit(solution)/shard_map/layer_backward/pallas_call | solution.py:651
  63.7 3.9 %unpack_heads.1 = (f32[128,2560]{1,0:T(8,128)}, f32[3,2560]{1,0:T(4,128)}) custom-call(f32[8,2,128,128]{3,2,1,0:T(8,128)} %get-tuple-element.5.v_any, f32[8,2,32,128]{3,2,1,0:T(8,128)} %get-tuple-element.6.qk_any, f32[8,2,8,256]{3,2,1,0:T(8,128)} %get-tuple-element.7.taps_ref), custom_call_target="tpu_custom_call" | custom-call | tf_op jit(solution)/shard_map/unpack_heads/pallas_call | solution.py:663

commit v6 on v5

--- a/solution.py
+++ b/solution.py
@@ -118,12 +118,12 @@
         for d in range(members):
             first = WIDTH * (d * hpd + h)
             sv[d, h] = p_ref[:, first + 32 : first + WIDTH]
-
-    for n in range(0, HEADS, 4):
-        four = [p_ref[:, WIDTH * k : WIDTH * k + 32] for k in range(n, n + 4)]
-        turned = jnp.concatenate(four, axis=1).T
-        for k in range(4):
-            sqk[(n + k) // hpd, (n + k) % hpd] = turned[32 * k : 32 * k + 32, :]
+        for d in range(0, members, 4):
+            firsts = [WIDTH * (k * hpd + h) for k in range(d, d + 4)]
+            turned = jnp.concatenate([p_ref[:, a : a + 32] for a in firsts], axis=1).T
+            for k in range(4):
+                sqk[d + k, h] = turned[32 * k : 32 * k + 32, :]
+
     pack(0)
     pl.semaphore_wait(barrier, members - 1 + groups - 1 + jnp.where(is_last, members - 1, 1))
 

time: 67.8 us -> 67.8 us (level)
  no operation moved by 1% of the time
where the time goes in v6:
time: 67.8 us; the launch traced here: 67.6 us
  Pallas kernels  66.9 us (99%)
    pallas_call x1, Pallas kernels, on_device(): pl.pallas_call(functools.partial(kernel, sub, side, groups, reach, 'seq',...  63 us
    pallas_call x1, Pallas kernels, on_device(): pl.pallas_call(functools.partial(unpack, hpd), out_shape=(jax.ShapeDtypeS...  3.9 us

profile of v6, /device:TPU:0, one launch (start us, length us, event | category | flops | bytes accessed | tf_op | source)
XLA Modules:
  0.0 67.6 jit_solution(1081812278836546304)
XLA Ops:
  0.6 63.0 %layer_backward.1 = (f32[8,2,128,128]{3,2,1,0:T(8,128)}, f32[8,2,32,128]{3,2,1,0:T(8,128)}, f32[8,2,8,256]{3,2,1,0:T(8,128)}) custom-call(s32[4]{0:T(128)} %docs_ref.1, f32[128,2560]{1,0:T(8,128)} %p_ref.1, f32[128,2048]{1,0:T(8,128)} %o_ref.1, f32[3,2560]{1,0:T(4,128)} %w_ref.1), custom_call_target="tpu_custom_call" | custom-call | tf_op jit(solution)/shard_map/layer_backward/pallas_call | solution.py:651
  63.7 3.9 %unpack_heads.1 = (f32[128,2560]{1,0:T(8,128)}, f32[3,2560]{1,0:T(4,128)}) custom-call(f32[8,2,128,128]{3,2,1,0:T(8,128)} %get-tuple-element.5.v_any, f32[8,2,32,128]{3,2,1,0:T(8,128)} %get-tuple-element.6.qk_any, f32[8,2,8,256]{3,2,1,0:T(8,128)} %get-tuple-element.7.taps_ref), custom_call_target="tpu_custom_call" | custom-call | tf_op jit(solution)/shard_map/unpack_heads/pallas_call | solution.py:663
